TPU v7x, 128 devices: a whole 4x4x4 slice. The times are simulated.
128 devices in a mesh: dp: 8 (over y, core), expert: 16 (over x, z).
Axes of the slice: x: 4, y: 4, z: 4, core: 2. Of those that a mesh axis runs over, the one named last changes fastest.
Arguments:
- grad_parts: bfloat16 [8, 64, 768, 2048], P('dp', None, 'expert'), may hold values from -80 to 80, as said below
- momentum: float32 [128, 768, 1024], P(('dp', 'expert')), may hold values from -6 to 6
Outputs:
- update: bfloat16 [64, 768, 2048], P(None, 'expert', 'dp')
- new_momentum: float32 [128, 768, 1024], P(('dp', 'expert'))
Inputs may be any that keep to these rules, and one draw needn't show every extreme that they name: `grad_parts`: real-valued gradient partials.
All inputs are finite; a program needn't handle non-finite values.
Results may differ from a plain program's by a relative error of at most 0.00105.
Values may be sent and summed in bfloat16 or wider, within the bound.
No kernel may reach another device: no remote copies, remote signals or barrier semaphores. Data moves between devices by JAX's collectives and lax.ppermute only.
A program may use at most 128 MiB of HBM per device.

v0:
```python
import math

import jax
import jax.numpy as jnp
from jax import lax
from jax.sharding import PartitionSpec as P

D = 2048
HID = 768
ITERS = 3


decay_rate = 0.95
norm_epsilon = 1e-07
rms_match = 0.2
lin_term = 3.4445
sq_term = -4.775
cube_term = 2.0315


def from_partner(block, axis, distance):
    count = lax.axis_size(axis)
    route = []
    for low in range(count):
        high = low | 1 << distance
        if high != low and high < count:
            route += [(low, high), (high, low)]
    return lax.ppermute(block, axis, route)


def product(left, right):
    return jnp.dot(left, right, precision=lax.Precision.HIGHEST, preferred_element_type=jnp.float32)


def pair_gram(block):
    local = product(block, block.T)
    return local + from_partner(local, "expert", 0)


def sweep(current, gram_block):
    poly = sq_term * gram_block + cube_term * product(gram_block, gram_block)
    return lin_term * current + product(poly, current)


def body(grad_parts, momentum):
    n_ex = lax.axis_size("expert")
    local_parts = grad_parts[0]
    mats, rows, width = local_parts.shape
    half = width // 2
    summed = lax.psum_scatter(
        local_parts.astype(jnp.float32), "dp", scatter_dimension=0, tiled=True
    )
    ordered = (
        summed.reshape(n_ex // 2, rows, 2, half).transpose(0, 2, 1, 3).reshape(n_ex, rows, half)
    )
    gradient = lax.all_to_all(ordered, "expert", split_axis=0, concat_axis=1, tiled=True)[0]
    renewed = decay_rate * momentum[0] + gradient
    nesterov = gradient + decay_rate * renewed
    squares = jnp.sum(nesterov * nesterov)
    total = jnp.sqrt(squares + from_partner(squares, "expert", 0))
    current = nesterov / (total + norm_epsilon)
    gram_block = pair_gram(current)
    for sweep_index in range(ITERS):
        if sweep_index > 0:
            gram_block = pair_gram(current)
        current = sweep(current, gram_block)
    update_half = (rms_match * math.sqrt(max(HID, D)) * current).astype(jnp.bfloat16)
    by_rows = lax.all_to_all(
        update_half.reshape(n_ex, rows, half), "expert", split_axis=0, concat_axis=0, tiled=True
    )
    joined = (
        by_rows.reshape(n_ex // 2, 2, rows, half)
        .transpose(0, 2, 1, 3)
        .reshape(n_ex // 2, rows, width)
    )
    update = lax.all_to_all(joined, "dp", split_axis=2, concat_axis=0, tiled=True)
    return (update, renewed[None])


def solution(mesh):
    placed = (P("dp", None, "expert", None), P(("dp", "expert"), None, None))
    return jax.shard_map(
        body,
        mesh=mesh,
        in_specs=placed,
        out_specs=(P(None, "expert", "dp"), P(("dp", "expert"), None, None)),
        check_vma=False,
    )
```

profile of v0, /device:TPU:0, one launch (start us, length us, event | category | flops | bytes accessed | tf_op | source)
XLA Modules:
  0.0 515.2 jit_solution(17453869891815268193)
XLA Ops:
  7.2 0.0 reduce-scatter.2.cloned.1.call-start
  7.2 14.5 %bitcast_convert_fusion = f32[64,48,2048]{2,1,0:T(8,128)} fusion(bf16[1,64,48,2048]{3,2,1,0:T(8,128)(2,1)} %param.2), kind=kLoop, calls=%fused_computation | loop fusion | flops 6291456 | bytes 37748736 | tf_op jit(solution)/shard_map/convert_element_type | solution.py:51
  21.7 0.0 reduce-scatter.2.cloned.1.call-update
  21.7 134.0 %reduce-scatter.2.cloned.1.call-done = f32[8,48,2048]{2,1,0:T(8,128)} async-done(((f32[64,48,2048]{2,1,0:T(8,128)}), f32[8,48,2048]{2,1,0:T(8,128)}) %reduce-scatter.2.cloned.1.call-update) | async-done | bytes 3145744 | tf_op jit(solution)/shard_map/reduce_scatter | solution.py:50
  155.7 2.3 fusion.42
  158.0 0.4 pad_maximum_fusion
  158.4 0.0 copy-start.1
  158.4 46.0 %all_to_all.32 = f32[16,48,1024]{2,1,0:T(8,128)S(1)} all-to-all(f32[16,48,1024]{2,1,0:T(8,128)S(1)} %bitcast.46), channel_id=1, replica_groups=mesh['dp'=8,'expert'=16] {'expert'}, dimensions={0} | all-to-all | bytes 6291456 | tf_op jit(solution)/shard_map/all_to_all | solution.py:56
  204.4 0.0 copy-done.1
  204.4 2.4 bitcast_add_fusion
  206.8 0.0 copy-start
  206.8 1.5 multiply_reduce_fusion
  208.3 0.1 copy-done
  208.4 0.8 collective-permute-start
  209.2 3.2 collective-permute-done
  213.6 3.0 broadcast_divide_fusion
  216.6 0.0 copy-start.2
  216.6 7.9 %fusion.43 = f32[768,768]{1,0:T(8,128)S(1)} fusion(f32[768,1024]{1,0:T(8,128)S(1)} %bitcast.43), kind=kOutput, calls=%fused_computation.48 | convolution fusion | flops 7247757312 | bytes 5505024 | tf_op jit(solution)/shard_map/dot_general | solution.py:32
  224.5 0.9 collective-permute-start.1
  225.4 0.0 copy-done.2
  225.4 0.8 fusion.2
  226.2 47.5 %collective-permute-done.1 = f32[768,768]{1,0:T(8,128)S(1)} collective-permute-done((f32[768,768]{1,0:T(8,128)S(1)}, f32[768,768]{1,0:T(8,128)S(1)}, u32[]{:S(2)}, u32[]{:S(2)}) %collective-permute-start.1) | collective-permute-done | bytes 2359328 | tf_op jit(solution)/shard_map/ppermute | solution.py:28
  273.6 6.0 %fusion.33 = f32[768,768]{1,0:T(8,128)S(1)} fusion(f32[768,768]{1,0:T(8,128)S(1)} %fusion.43, f32[768,768]{1,0:T(8,128)S(1)} %collective-permute-done.1), kind=kOutput, calls=%fused_computation.38 | convolution fusion | flops 5436407808 | bytes 7077888 | tf_op jit(solution)/shard_map/dot_general | solution.py:32
  279.7 8.5 %multiply_add_fusion.1 = f32[768,1024]{1,0:T(8,128)S(1)} fusion(f32[768,1024]{1,0:T(8,128)S(1)} %fusion.2, f32[768,768]{1,0:T(8,128)S(1)} %fusion.33, f32[768,768]{1,0:T(8,128)S(1)} %fusion.43, f32[768,768]{1,0:T(8,128)S(1)} %collective-permute-done.1), kind=kOutput, calls=%fused_computation.9 | convolution fusion | flops 7251689472 | bytes 13369344 | tf_op jit(solution)/shard_map/dot_general | solution.py:32
  288.1 7.9 %fusion.44 = f32[768,768]{1,0:T(8,128)S(1)} fusion(f32[768,1024]{1,0:T(8,128)S(1)} %multiply_add_fusion.1), kind=kOutput, calls=%fused_computation.49 | convolution fusion | flops 7247757312 | bytes 5505024 | tf_op jit(solution)/shard_map/dot_general | solution.py:32
  296.0 0.8 collective-permute-start.2
  296.8 47.4 %collective-permute-done.2 = f32[768,768]{1,0:T(8,128)S(1)} collective-permute-done((f32[768,768]{1,0:T(8,128)S(1)}, f32[768,768]{1,0:T(8,128)S(1)}, u32[]{:S(2)}, u32[]{:S(2)}) %collective-permute-start.2) | collective-permute-done | bytes 2359328 | tf_op jit(solution)/shard_map/ppermute | solution.py:28
  344.2 6.0 %fusion.30 = f32[768,768]{1,0:T(8,128)S(1)} fusion(f32[768,768]{1,0:T(8,128)S(1)} %fusion.44, f32[768,768]{1,0:T(8,128)S(1)} %collective-permute-done.2), kind=kOutput, calls=%fused_computation.35 | convolution fusion | flops 5436407808 | bytes 7077888 | tf_op jit(solution)/shard_map/dot_general | solution.py:32
  350.2 8.2 %multiply_add_fusion = f32[768,1024]{1,0:T(8,128)S(1)} fusion(f32[768,1024]{1,0:T(8,128)S(1)} %multiply_add_fusion.1, f32[768,768]{1,0:T(8,128)S(1)} %fusion.30, f32[768,768]{1,0:T(8,128)S(1)} %fusion.44, f32[768,768]{1,0:T(8,128)S(1)} %collective-permute-done.2), kind=kOutput, calls=%fused_computation.8 | convolution fusion | flops 7251689472 | bytes 13369344 | tf_op jit(solution)/shard_map/dot_general | solution.py:32
  358.4 7.9 %fusion.45 = f32[768,768]{1,0:T(8,128)S(1)} fusion(f32[768,1024]{1,0:T(8,128)S(1)} %multiply_add_fusion), kind=kOutput, calls=%fused_computation.50 | convolution fusion | flops 7247757312 | bytes 5505024 | tf_op jit(solution)/shard_map/dot_general | solution.py:32
  366.3 1.5 collective-permute-start.3
  367.8 46.4 %collective-permute-done.3 = f32[768,768]{1,0:T(8,128)S(1)} collective-permute-done((f32[768,768]{1,0:T(8,128)S(1)}, f32[768,768]{1,0:T(8,128)S(1)}, u32[]{:S(2)}, u32[]{:S(2)}) %collective-permute-start.3) | collective-permute-done | bytes 2359328 | tf_op jit(solution)/shard_map/ppermute | solution.py:28
  414.3 6.1 %fusion.27 = f32[768,768]{1,0:T(8,128)S(1)} fusion(f32[768,768]{1,0:T(8,128)S(1)} %fusion.45, f32[768,768]{1,0:T(8,128)S(1)} %collective-permute-done.3), kind=kOutput, calls=%fused_computation.32 | convolution fusion | flops 5436407808 | bytes 7077888 | tf_op jit(solution)/shard_map/dot_general | solution.py:32
  420.4 8.5 %multiply_convert_fusion = bf16[768,1024]{1,0:T(8,128)(2,1)S(1)} fusion(f32[768,1024]{1,0:T(8,128)S(1)} %multiply_add_fusion, f32[768,768]{1,0:T(8,128)S(1)} %fusion.27, f32[768,768]{1,0:T(8,128)S(1)} %fusion.45, f32[768,768]{1,0:T(8,128)S(1)} %collective-permute-done.3), kind=kOutput, calls=%fused_computation.7 | convolution fusion | flops 7253262336 | bytes 11796480 | tf_op jit(solution)/shard_map/dot_general | solution.py:32
  428.9 27.6 %all_to_all.33 = bf16[16,48,1024]{2,1,0:T(8,128)(2,1)S(1)} all-to-all(bf16[16,48,1024]{2,1,0:T(8,128)(2,1)S(1)} %bitcast.48), channel_id=1, replica_groups=mesh['dp'=8,'expert'=16] {'expert'}, dimensions={0} | all-to-all | bytes 3145728 | tf_op jit(solution)/shard_map/all_to_all | solution.py:68
  456.5 4.3 copy.10
  460.8 8.1 %reshape.38 = bf16[8,2,49152]{2,1,0:T(2,128)(2,1)S(1)} reshape(bf16[2048,8,48]{2,1,0:T(8,128)(2,1)} %bitcast.44) | data formatting | bytes 3145728
  468.8 28.3 %all_to_all.34 = bf16[8,2,49152]{2,1,0:T(2,128)(2,1)S(1)} all-to-all(bf16[8,2,49152]{2,1,0:T(2,128)(2,1)S(1)} %reshape.38), channel_id=1, replica_groups=mesh['dp'=8,'expert'=16] {'dp'}, dimensions={0} | all-to-all | bytes 3145728 | tf_op jit(solution)/shard_map/all_to_all | solution.py:76
  497.1 5.8 %reshape.39 = bf16[2048,8,48]{2,1,0:T(8,128)(2,1)} reshape(bf16[8,2,49152]{2,1,0:T(2,128)(2,1)S(1)} %all_to_all.34) | data formatting | bytes 3145728
  502.9 5.0 copy.9
Async XLA Ops:
  7.2 148.5 %reduce-scatter.2.cloned.1.call-start = ((), (), s32[]{:S(2)}) async-start(), calls=%async_computation.4 | async-start | bytes 28311552 | tf_op jit(solution)/shard_map/reduce_scatter | solution.py:50
  158.4 46.0 %copy-start.1 = (f32[1,768,1024]{2,1,0:T(8,128)S(1)}, f32[1,768,1024]{2,1,0:T(8,128)}, u32[]{:S(2)}) copy-start(f32[1,768,1024]{2,1,0:T(8,128)} %param.3) | copy-start | bytes 9437188
  206.8 1.6 copy-start
  208.4 4.0 collective-permute-start
  216.6 8.8 %copy-start.2 = (f32[1,768,1024]{2,1,0:T(8,128)S(1)}, f32[1,768,1024]{2,1,0:T(8,128)}, u32[]{:S(2)}) copy-start(f32[1,768,1024]{2,1,0:T(8,128)} %param.3) | copy-start | bytes 9437188
  224.5 49.2 %collective-permute-start.1 = (f32[768,768]{1,0:T(8,128)S(1)}, f32[768,768]{1,0:T(8,128)S(1)}, u32[]{:S(2)}, u32[]{:S(2)}) collective-permute-start(f32[768,768]{1,0:T(8,128)S(1)} %fusion.43), channel_id=1, source_target_pairs={{0,1},{1,0},{2,3},{3,2},{4,5},{5,4},{6,7},{7,6},{8,9},{9,8},{10,11... | collective-permute-start | bytes 7077896 | tf_op jit(solution)/shard_map/ppermute | solution.py:28
  296.0 48.2 %collective-permute-start.2 = (f32[768,768]{1,0:T(8,128)S(1)}, f32[768,768]{1,0:T(8,128)S(1)}, u32[]{:S(2)}, u32[]{:S(2)}) collective-permute-start(f32[768,768]{1,0:T(8,128)S(1)} %fusion.44), channel_id=1, source_target_pairs={{0,1},{1,0},{2,3},{3,2},{4,5},{5,4},{6,7},{7,6},{8,9},{9,8},{10,11... | collective-permute-start | bytes 7077896 | tf_op jit(solution)/shard_map/ppermute | solution.py:28
  366.3 48.0 %collective-permute-start.3 = (f32[768,768]{1,0:T(8,128)S(1)}, f32[768,768]{1,0:T(8,128)S(1)}, u32[]{:S(2)}, u32[]{:S(2)}) collective-permute-start(f32[768,768]{1,0:T(8,128)S(1)} %fusion.45), channel_id=1, source_target_pairs={{0,1},{1,0},{2,3},{3,2},{4,5},{5,4},{6,7},{7,6},{8,9},{9,8},{10,11... | collective-permute-start | bytes 7077896 | tf_op jit(solution)/shard_map/ppermute | solution.py:28
Sparse Core Ops, SparseCore 0:
  21.8 133.8 reduce-scatter.1
where the time goes:
time: 519 us; the launch traced here: 515 us
  waiting for transfers between devices  278 us (54%)
  blocking collectives  102 us (20%)
  matrix products  67 us (13%)
  local copies, waits for them, and re-layouts  25.5 us (5%)
  other arithmetic  22.5 us (4%)
  between operations  15.9 us (3%)
    ppermute x4, waiting for transfers between devices, from_partner(): return lax.ppermute(block, axis, route)  144 us
    reduce_scatter x1, waiting for transfers between devices, body(): lax.psum_scatter(local_parts.astype(jnp.float32), 'dp', scatter_dimension...  134 us
    dot_general x9, matrix products, product(): jnp.dot(left, right, precision=lax.Precision.HIGHEST, preferred_element_t...  67 us
    all_to_all x1, blocking collectives, body(): lax.all_to_all(ordered, 'expert', split_axis=0, concat_axis=1, tiled=True)  46 us
    all_to_all x1, blocking collectives, body(): lax.all_to_all(joined, 'dp', split_axis=2, concat_axis=0, tiled=True)  28.3 us
    all_to_all x1, blocking collectives, body(): lax.all_to_all(update_half.reshape(n_ex, rows, half), 'expert', split_axi...  27.6 us
    convert_element_type x1, other arithmetic, body(): local_parts.astype(jnp.float32)  14.5 us
    unnamed x8, local copies, waits for them, and re-layouts  13.9 us
  transfers between devices with their start and end apart: 5, of which 5 were waited for; matrix products, arithmetic and copies ran while one was open for 0% of the time, Pallas kernels for 0%

commit v1 on v0

v1 whole, which is shorter than its diff:
```python
import functools
import math

import jax
import jax.numpy as jnp
from jax import lax
from jax.experimental import pallas as pl
from jax.experimental.pallas import tpu as pltpu
from jax.sharding import PartitionSpec as P

D = 2048
HID = 768
HALF = D // 2
ROWS = 48
LANES = 128

decay_rate = 0.95
norm_epsilon = 1e-07
rms_match = 0.2
lin_term = 3.4445
sq_term = -4.775
cube_term = 2.0315

WIDTHS = (256, 256, 256, 256)
OFFSETS = tuple(sum(WIDTHS[:c]) for c in range(len(WIDTHS)))

F32 = jnp.float32
BF16 = jnp.bfloat16
MIB = 1 << 20


def call(kernel, inputs, in_specs, out_specs, out_shape, name,
         after=(), grid=(), where=None, aliases=None, scratch=(), micros=2.0):
    n, extra, outs = len(inputs), len(after), len(out_shape)
    lead = 0 if where is None else 1

    def run(*refs):
        first = lead + n + extra
        refs[first + outs][...] = jnp.zeros((8, LANES), F32)
        kernel(*refs[: lead + n], *refs[first : first + outs], *refs[first + outs + 1 :])

    spec = pltpu.PrefetchScalarGridSpec(
        num_scalar_prefetch=lead,
        grid=grid,
        in_specs=list(in_specs) + [pl.BlockSpec(memory_space=pl.ANY)] * extra,
        out_specs=list(out_specs) + [pl.BlockSpec((8, LANES), lambda *_: (0, 0))],
        scratch_shapes=scratch,
    )
    return pl.pallas_call(
        run,
        grid_spec=spec,
        out_shape=list(out_shape) + [jax.ShapeDtypeStruct((8, LANES), F32)],
        input_output_aliases={lead + k: v for k, v in (aliases or {}).items()},
        compiler_params=pltpu.CompilerParams(vmem_limit_bytes=50 * MIB),
        cost_estimate=pl.CostEstimate(
            flops=0, bytes_accessed=int(micros * 10), transcendentals=0
        ),
        name=name,
    )(*(() if where is None else (where,)), *inputs, *after)


def split(x):
    high = x.astype(BF16)
    return high, (x - high.astype(F32)).astype(BF16)


NN = (((1,), (0,)), ((), ()))
NT = (((1,), (1,)), ((), ()))


def dot3(ah, al, bh, bl, dims):
    dot = functools.partial(lax.dot_general, dimension_numbers=dims, preferred_element_type=F32)
    return dot(ah, bh) + (dot(ah, bl) + dot(al, bh))


def step_width(c):
    return math.gcd(WIDTHS[c], OFFSETS[c], 256)


def pack_kernel(where, g_ref, out_ref):
    out_ref[...] = g_ref[:, 0]


def pack(where, grads, c, after):
    step = step_width(c)
    n, first, half = WIDTHS[c] // step, OFFSETS[c] // step, HALF // step
    return call(
        pack_kernel,
        [grads],
        [
            pl.BlockSpec(
                (4, 1, 8, ROWS, step), lambda h, i, s: (0, 1 - s[0], 0, 0, h * half + first + i)
            )
        ],
        [pl.BlockSpec((4, 8, ROWS, step), lambda h, i, s: (0, 0, 0, h * n + i))],
        [jax.ShapeDtypeStruct((4, 8, ROWS, 2 * WIDTHS[c]), BF16)],
        "pack", after, (2, n), where, micros=2.0 * WIDTHS[c] / 256,
    )


def pair_sum_kernel(where, g_ref, r_ref, up_ref, down_ref, acc_ref, own_ref):
    y = where[1]

    def total(k, rows):
        k = lax.rem(k, 4)
        return g_ref[k, 0, rows].astype(F32) + r_ref[k, rows].astype(F32)

    for rows, up, down, acc in ((slice(0, 4), 2, 3, 1), (slice(4, 8), 1, 2, 3)):
        own_ref[rows] = total(y, rows)
        up_ref[rows] = total(y + up, rows)
        down_ref[rows] = total(y + down, rows)
        acc_ref[rows] = total(y + acc, rows)


def pair_sum(where, grads, received, c, after):
    step = step_width(c)
    n, first, half = WIDTHS[c] // step, OFFSETS[c] // step, HALF // step
    return call(
        pair_sum_kernel,
        [grads, received],
        [
            pl.BlockSpec(
                (4, 1, 8, ROWS, step), lambda h, i, s: (0, s[0], 0, 0, h * half + first + i)
            ),
            pl.BlockSpec((4, 8, ROWS, step), lambda h, i, s: (0, 0, 0, h * n + i)),
        ],
        [pl.BlockSpec((8, ROWS, step), lambda h, i, s: (0, 0, h * n + i))] * 4,
        [jax.ShapeDtypeStruct((8, ROWS, 2 * WIDTHS[c]), F32)] * 4,
        "pair_sum", after, (2, n), where, micros=4.0 * WIDTHS[c] / 256,
    )


def relay_kernel(acc_up, u1_ref, acc_down, d1_ref, up_ref, down_ref):
    up_ref[...] = acc_up[...] + u1_ref[...]
    down_ref[...] = acc_down[...] + d1_ref[...]


def relay(acc, u1, d1, w, after):
    block = (2, ROWS, 2 * w)
    low = pl.BlockSpec(block, lambda i: (i, 0, 0))
    high = pl.BlockSpec(block, lambda i: (i + 2, 0, 0))
    return call(
        relay_kernel,
        [acc, u1, acc, d1],
        [low, low, high, high],
        [low, low],
        [jax.ShapeDtypeStruct((4, ROWS, 2 * w), F32)] * 2,
        "relay", after, (2,), micros=1.0,
    )


def finish_kernel(own_ref, d1_ref, u2_ref, u1_ref, d2_ref, out_ref):
    def write(a_ref, b_ref):
        total = own_ref[...] + (a_ref[...] + b_ref[...])
        for j in range(4):
            out_ref[2 * j] = total[j]
            out_ref[2 * j + 1] = total[j]

    pl.when(pl.program_id(0) == 0)(lambda: write(d1_ref, u2_ref))
    pl.when(pl.program_id(0) == 1)(lambda: write(u1_ref, d2_ref))


def finish(own, d1, u2, u1, d2, w, after):
    block = (4, ROWS, 2 * w)
    held = pl.BlockSpec(block, lambda i: (0, 0, 0))
    return call(
        finish_kernel,
        [own, d1, u2, u1, d2],
        [
            pl.BlockSpec(block, lambda i: (i, 0, 0)),
            held,
            held,
            pl.BlockSpec(block, lambda i: (1, 0, 0)),
            held,
        ],
        [pl.BlockSpec((8, ROWS, 2 * w), lambda i: (i, 0, 0))],
        [jax.ShapeDtypeStruct((16, ROWS, 2 * w), F32)],
        "finish", after, (2,), micros=1.0,
    )


def step_of(gradient, momentum):
    renewed = decay_rate * momentum + gradient
    return renewed, gradient + decay_rate * renewed


def add_gram(total_ref, before_ref, own, other):
    high, low = split(jnp.concatenate([own, other], axis=1))
    for i in range(3):
        rows = slice(i * 256, (i + 1) * 256)
        block = dot3(high[rows], low[rows], high, low, NT)
        total_ref[rows] = block if before_ref is None else before_ref[rows] + block


def nesterov_kernel(where, g_ref, gp_ref, m_ref, mp_ref, *refs):
    new_ref, own_ref, other_ref, total_ref = refs[-4:]
    new_ref[...], own = step_of(g_ref[...], m_ref[...])
    other = step_of(gp_ref[...], mp_ref[...])[1]
    own_ref[...], other_ref[...] = own, other
    first = pl.program_id(0) == 0
    before = refs[0] if len(refs) > 4 else None
    pl.when(first)(lambda: add_gram(total_ref, before, own, other))
    pl.when(jnp.logical_not(first))(lambda: add_gram(total_ref, total_ref, own, other))


def nesterov(where, gradient, momentum, partner, state, c, after):
    step = step_width(c)
    n, first = WIDTHS[c] // step, OFFSETS[c] // step
    block = (HID, step)
    mine = pl.BlockSpec(block, lambda i, s: (0, s[2] * n + i))
    theirs = pl.BlockSpec(block, lambda i, s: (0, (1 - s[2]) * n + i))
    place = pl.BlockSpec(block, lambda i, s: (0, first + i))
    whole = pl.BlockSpec((HID, HID), lambda i, s: (0, 0))
    wide = jax.ShapeDtypeStruct((HID, HALF), F32)
    carried = [] if state is None else [state[3], state[0], state[1], state[2]]
    return call(
        nesterov_kernel,
        [gradient, gradient, momentum, partner] + carried,
        [mine, theirs, place, place]
        + ([whole] + [pl.BlockSpec(memory_space=pl.ANY)] * 3 if carried else []),
        [place, place, place, whole],
        [wide, wide, wide, jax.ShapeDtypeStruct((HID, HID), F32)],
        "nesterov", after, (n,), where,
        aliases={5: 0, 6: 1, 7: 2} if carried else {},
        micros=6.0,
    )


def solve_kernel(where, g_ref, gp_ref, m_ref, mp_ref, before_ref, *refs):
    own_refs, other_refs, refs = refs[:4], refs[4:8], refs[9:]
    new_ref, out_ref, gram_ref, last_own, last_other, *scratch = refs
    h = where[2]
    pairs = [scratch[2 * i : 2 * i + 2] for i in range(4)]

    new_ref[...], own = step_of(g_ref[...], m_ref[...])
    other = step_of(gp_ref[...], mp_ref[...])[1]
    last_own[...], last_other[...] = own, other
    add_gram(gram_ref, before_ref, own, other)

    eye = lax.broadcasted_iota(jnp.int32, (HID, HID), 0) == lax.broadcasted_iota(
        jnp.int32, (HID, HID), 1
    )
    gram_block = gram_ref[...]
    squares = jnp.sum(jnp.where(eye, gram_block, 0.0), axis=(0, 1), keepdims=True)
    inverse = 1.0 / (jnp.sqrt(squares) + norm_epsilon)
    a, p, s, q = pairs
    a[0][...], a[1][...] = split(gram_block * (inverse * inverse))

    def multiply(x, y, to, poly=None):
        for i in range(3):
            rows = slice(i * 256, (i + 1) * 256)
            for j in range(i, 3):
                cols = slice(j * 256, (j + 1) * 256)
                value = dot3(x[0][rows], x[1][rows], y[0][:, cols], y[1][:, cols], NN)
                if poly is not None:
                    base = poly[0][rows, cols].astype(F32) + poly[1][rows, cols].astype(F32)
                    value = sq_term * base + cube_term * value
                    if i == j:
                        value = value + jnp.where(eye[:256, :256], lin_term, 0.0)
                high, low = split(value)
                to[0][rows, cols], to[1][rows, cols] = high, low
                if j > i:
                    to[0][cols, rows], to[1][cols, rows] = high.T, low.T

    multiply(a, a, p, a)
    multiply(p, a, s)
    multiply(p, s, a)
    multiply(a, a, s, a)
    multiply(s, p, q)
    multiply(s, a, p)
    multiply(s, p, a)
    multiply(a, a, s, a)
    multiply(s, q, p)

    scale = inverse * (rms_match * math.sqrt(max(HID, D)))
    in_last = 256 * 3 + LANES * h >= OFFSETS[-1]
    column = pl.multiple_of(256 * 3 + LANES * h - OFFSETS[-1], LANES) if WIDTHS[-1] > LANES else 0
    for k in range(4):
        own, other = own_refs[k][...], other_refs[k][...]
        if k == 3:
            here = pl.ds(column, LANES)
            own = jnp.where(in_last, last_own[:, here], own)
            other = jnp.where(in_last, last_other[:, here], other)
        high, low = split(jnp.concatenate([own, other], axis=1))
        for i in range(3):
            rows = slice(i * 256, (i + 1) * 256)
            value = dot3(p[0][rows], p[1][rows], high, low, NN) * scale
            value = value.astype(BF16)
            out_ref[4 * h + k, rows] = value[:, :LANES]
            out_ref[4 * (1 - h) + k, rows] = value[:, LANES:]


def solve(where, gradient, momentum, partner, state):
    c = len(WIDTHS) - 1
    w = WIDTHS[c]
    block = (HID, w)
    place = pl.BlockSpec(block, lambda i, s: (0, OFFSETS[c] // w))
    whole = pl.BlockSpec((HID, HID), lambda i, s: (0, 0))
    columns = [
        pl.BlockSpec((HID, LANES), lambda i, s, k=k: (0, 2 * k + s[2])) for k in range(4)
    ]
    renewed, own, other, total = state
    return call(
        solve_kernel,
        [gradient, gradient, momentum, partner, total] + [own] * 4 + [other] * 4 + [renewed],
        [
            pl.BlockSpec(block, lambda i, s: (0, s[2])),
            pl.BlockSpec(block, lambda i, s: (0, 1 - s[2])),
            place,
            place,
            whole,
            *columns,
            *columns,
            pl.BlockSpec(memory_space=pl.ANY),
        ],
        [place, pl.BlockSpec((8, HID, LANES), lambda i, s: (0, 0, 0))],
        [
            jax.ShapeDtypeStruct((HID, HALF), F32),
            jax.ShapeDtypeStruct((8, HID, LANES), BF16),
        ],
        "solve", (), (1,), where,
        aliases={13: 0},
        scratch=[pltpu.VMEM((HID, HID), F32)]
        + [pltpu.VMEM(block, F32)] * 2
        + [pltpu.VMEM((HID, HID), BF16)] * 8,
        micros=40.0,
    )


def join_kernel(x_ref, out_ref):
    for h in range(2):
        out_ref[:, :, h * LANES : (h + 1) * LANES] = x_ref[:, h]


def join(blocks):
    out, _ = call(
        join_kernel,
        [blocks],
        [pl.BlockSpec((16, 2, ROWS, LANES), lambda i: (i, 0, 0, 0))],
        [pl.BlockSpec((16, ROWS, 2 * LANES), lambda i: (i, 0, 0))],
        [jax.ShapeDtypeStruct((64, ROWS, 2 * LANES), BF16)],
        "join", grid=(4,),
    )
    return out


def body(grad_parts, momentum):
    dp, ex = lax.axis_index("dp"), lax.axis_index("expert")
    where = jnp.stack([dp % 2, dp // 2, ex % 2]).astype(jnp.int32)
    grads = grad_parts.reshape(4, 2, 8, ROWS, D)
    momentum = momentum[0]
    core = [(i, i ^ 1) for i in range(8)]
    upward = [(i, (i + 2) % 8) for i in range(8)]
    downward = [(i, (i - 2) % 8) for i in range(8)]
    partner = [(i, i ^ 1) for i in range(16)]
    n = len(WIDTHS)
    theirs = lax.ppermute(momentum, "expert", partner)
    received, sums, first, second, moved, token = ({} for _ in range(6))

    def after(*steps):
        return [token[step] for step in steps if step in token]

    def do_pack(c, *waits):
        out, token["pack", c] = pack(where, grads, c, after(*waits))
        received[c] = lax.ppermute(out, "dp", core)

    def do_sum(c, *waits):
        *sums[c], token["sum", c] = pair_sum(where, grads, received[c], c, after(*waits))
        up, down = sums[c][:2]
        first[c] = (lax.ppermute(up, "dp", upward), lax.ppermute(down, "dp", downward))

    def do_relay(c, *waits):
        up, down, token["relay", c] = relay(sums[c][2], *first[c], WIDTHS[c], after(*waits))
        second[c] = (lax.ppermute(up, "dp", upward), lax.ppermute(down, "dp", downward))

    def do_finish(c, *waits, arrays=()):
        out, token["finish", c] = finish(
            sums[c][3], first[c][1], second[c][0], first[c][0], second[c][1], WIDTHS[c],
            after(*waits) + list(arrays),
        )
        out = lax.all_to_all(out, "expert", split_axis=0, concat_axis=0, tiled=True)
        moved[c] = out.reshape(HID, -1)

    def do_nesterov(c, *waits):
        *state[:], token["nesterov", c] = nesterov(
            where, moved[c], momentum, theirs, state or None, c, after(*waits)
        )

    state = []
    do_pack(0)
    do_pack(1)
    do_sum(0)
    do_sum(1)
    do_pack(2)
    do_relay(0, ("sum", 1), ("pack", 2))
    do_sum(2, ("relay", 0))
    for c in range(n):
        if c + 3 < n:
            do_pack(c + 3, ("sum", c + 2))
        if c + 1 < n:
            do_relay(c + 1, ("sum", c + 2), ("pack", c + 3), ("finish", c - 1))
        if c + 3 < n:
            do_sum(c + 3, ("relay", c + 1))
        last = () if c == n - 1 else (("nesterov", c - 2),)
        do_finish(c, ("sum", c + 3), ("relay", c + 1), *last, arrays=[theirs] if c == 1 else ())
        if c > 0:
            do_nesterov(c - 1, ("finish", c))
    renewed, update, _ = solve(where, moved[n - 1], momentum, theirs, state)
    update = lax.all_to_all(
        update.reshape(128, ROWS, LANES), ("dp", "expert"), split_axis=0, concat_axis=0, tiled=True
    )
    return join(update.reshape(64, 2, ROWS, LANES)), renewed[None]


def solution(mesh):
    return jax.shard_map(
        body,
        mesh=mesh,
        in_specs=(P("dp", None, "expert", None), P(("dp", "expert"), None, None)),
        out_specs=(P(None, "expert", "dp"), P(("dp", "expert"), None, None)),
        check_vma=False,
    )
```

time: 519 us -> 271 us (0.52)
  waiting for transfers between devices: 278 us -> 80 us
  Pallas kernels: 0 us -> 80 us
  blocking collectives: 102 us -> 31.7 us
  matrix products: 67 us -> 0 us
  starting transfers between devices: 4.02 us -> 54.3 us
  other arithmetic: 22.5 us -> 0.08 us
  between operations: 15.9 us -> 1.17 us
    reduce_scatter x1 -> x0, waiting for transfers between devices: 134 us -> none  [body(): lax.psum_scatter(local_parts.astype(jnp.float32), 'dp', scatter_dimension...]
    pallas_call x0 -> x21, Pallas kernels: none -> 80 us  [call(): pl.pallas_call(run, grid_spec=spec, out_shape=list(out_shape) + [jax.Shap...]
    all_to_all x3 -> x1, blocking collectives: 102 us -> 31.7 us  [body(): lax.all_to_all(update.reshape(128, ROWS, LANES), ('dp', 'expert'), split_...]
    ppermute x4 -> x21, waiting for transfers between devices: 144 us -> 74.9 us  [the longest x4 49.1 us: do_sum(): lax.ppermute(up, 'dp', upward)]
    dot_general x9 -> x0, matrix products: 67 us -> none  [product(): jnp.dot(left, right, precision=lax.Precision.HIGHEST, preferred_element_t...]
    all_to_all x0 -> x4, starting transfers between devices: none -> 26.5 us  [do_finish(): out = lax.all_to_all(out, 'expert', split_axis=0, concat_axis=0, tiled=True)]
    ppermute x4 -> x21, starting transfers between devices: 3.98 us -> 27.7 us  [the longest x4 11.5 us: do_relay(): lax.ppermute(down, 'dp', downward)]
    convert_element_type x1 -> x0, other arithmetic: 14.5 us -> none  [body(): local_parts.astype(jnp.float32)]
  transfers between devices with their start and end apart: 5 -> 25, of which waited for: 5 -> 10; matrix products, arithmetic and copies ran while one was open for 0% -> 0% of each run, Pallas kernels for 0% -> 15%
where the time goes in v1:
time: 271 us; the launch traced here: 268 us
  Pallas kernels  80 us (30%)
  waiting for transfers between devices  80 us (30%)
  starting transfers between devices  54.3 us (20%)
  blocking collectives  31.7 us (12%)
  local copies, waits for them, and re-layouts  20.4 us (8%)
    pallas_call x21, Pallas kernels, call(): pl.pallas_call(run, grid_spec=spec, out_shape=list(out_shape) + [jax.Shap...  80 us
    ppermute x4, waiting for transfers between devices, do_sum(): lax.ppermute(up, 'dp', upward)  49.1 us
    all_to_all x1, blocking collectives, body(): lax.all_to_all(update.reshape(128, ROWS, LANES), ('dp', 'expert'), split_...  31.7 us
    all_to_all x4, starting transfers between devices, do_finish(): out = lax.all_to_all(out, 'expert', split_axis=0, concat_axis=0, tiled=True)  26.5 us
    unnamed x64, local copies, waits for them, and re-layouts  20.4 us
    ppermute x4, waiting for transfers between devices, do_sum(): lax.ppermute(down, 'dp', downward)  14.5 us
    ppermute x4, starting transfers between devices, do_relay(): lax.ppermute(down, 'dp', downward)  11.5 us
    ppermute x4, waiting for transfers between devices, do_relay(): lax.ppermute(up, 'dp', upward)  9.63 us
  transfers between devices with their start and end apart: 25, of which 10 were waited for; matrix products, arithmetic and copies ran while one was open for 0% of the time, Pallas kernels for 15%

profile of v1, /device:TPU:0, one launch (start us, length us, event | category | flops | bytes accessed | tf_op | source)
XLA Modules:
  0.0 267.7 jit_solution(8298284006818594350)
XLA Ops:
  0.7 2.7 %pack.5 = (bf16[4,8,48,512]{3,2,1,0:T(8,128)(2,1)S(1)}, f32[8,128]{1,0:T(8,128)}) custom-call(s32[3]{0:T(128)S(1)} %pad_add_fusion.refs_0_, bf16[4,2,8,48,2048]{4,3,2,1,0:T(8,128)(2,1)} %bitcast.20), custom_call_target="tpu_custom_call" | custom-call | bytes 20 | tf_op jit(solution)/shard_map/pack/pallas_call | solution.py:49
  3.4 2.7 pack.6
  6.6 2.1 pack.4
  10.0 3.3 %pair_sum.4 = (f32[8,48,512]{2,1,0:T(8,128)S(1)}, f32[8,48,512]{2,1,0:T(8,128)S(1)}, f32[8,48,512]{2,1,0:T(8,128)S(1)}, f32[8,48,512]{2,1,0:T(8,128)S(1)}, f32[8,128]{1,0:T(8,128)}) custom-call(s32[3]{0:T(128)S(1)} %pad_add_fusion.refs_0_, bf16[4,2,8,48,2048]{4,3,2,1,0:T(8,128)(2,1)} %bitcast.23, bf16[4,8,48,512]{3,2,1,0:T(8,128)(2,1)} %copy-done.31), custom_call_target="tpu_custom_call" | custom-call | bytes 40 | tf_op jit(solution)/shard_map/pair_sum/pallas_call | solution.py:49
  13.3 1.7 collective-permute-start.2
  14.9 1.6 collective-permute-start.3
  16.5 2.0 collective-permute-start.16
  18.5 2.7 %pair_sum.5 = (f32[8,48,512]{2,1,0:T(8,128)S(1)}, f32[8,48,512]{2,1,0:T(8,128)S(1)}, f32[8,48,512]{2,1,0:T(8,128)S(1)}, f32[8,48,512]{2,1,0:T(8,128)S(1)}, f32[8,128]{1,0:T(8,128)S(1)}) custom-call(s32[3]{0:T(128)S(1)} %pad_add_fusion.refs_0_, bf16[4,2,8,48,2048]{4,3,2,1,0:T(8,128)(2,1)} %bitcast.24, bf16[4,8,48,512]{3,2,1,0:T(8,128)(2,1)} %collective-permute-done.4.refs_2_), custom_call_target="tpu_custom_call" | custom-call | bytes 40 | tf_op jit(solution)/shard_map/pair_sum/pallas_call | solution.py:49
  22.1 12.4 %collective-permute-done.2.refs_1_.refs_3_ = f32[8,48,512]{2,1,0:T(8,128)S(1)} collective-permute-done((f32[8,48,512]{2,1,0:T(8,128)S(1)}, f32[8,48,512]{2,1,0:T(8,128)S(1)}, u32[]{:S(2)}, u32[]{:S(2)}) %collective-permute-start.2) | collective-permute-done | bytes 786464 | tf_op jit(solution)/shard_map/ppermute | solution.py:370
  35.8 2.7 %pair_sum.6 = (f32[8,48,512]{2,1,0:T(8,128)S(1)}, f32[8,48,512]{2,1,0:T(8,128)S(1)}, f32[8,48,512]{2,1,0:T(8,128)S(1)}, f32[8,48,512]{2,1,0:T(8,128)S(1)}, f32[8,128]{1,0:T(8,128)S(1)}) custom-call(s32[3]{0:T(128)S(1)} %pad_add_fusion.refs_0_, bf16[4,2,8,48,2048]{4,3,2,1,0:T(8,128)(2,1)} %bitcast.25, bf16[4,8,48,512]{3,2,1,0:T(8,128)(2,1)} %copy-done.29, ...), custom_call_target="tpu_custom_call" | custom-call | bytes 40 | tf_op jit(solution)/shard_map/pair_sum/pallas_call | solution.py:49
  40.4 2.1 pack.7
  42.6 1.6 collective-permute-start.6
  44.2 1.7 collective-permute-start.7
  46.3 18.0 %collective-permute-done.6.refs_1_.refs_3_ = f32[8,48,512]{2,1,0:T(8,128)S(1)} collective-permute-done((f32[8,48,512]{2,1,0:T(8,128)S(1)}, f32[8,48,512]{2,1,0:T(8,128)S(1)}, u32[]{:S(2)}, u32[]{:S(2)}) %collective-permute-start.6) | collective-permute-done | bytes 786464 | tf_op jit(solution)/shard_map/ppermute | solution.py:370
  64.2 1.7 collective-permute-start.15
  67.1 1.1 copy-done.30
  68.2 2.7 %pair_sum.7 = (f32[8,48,512]{2,1,0:T(8,128)S(1)}, f32[8,48,512]{2,1,0:T(8,128)S(1)}, f32[8,48,512]{2,1,0:T(8,128)S(1)}, f32[8,48,512]{2,1,0:T(8,128)S(1)}, f32[8,128]{1,0:T(8,128)S(1)}) custom-call(s32[3]{0:T(128)S(1)} %pad_add_fusion.refs_0_, bf16[4,2,8,48,2048]{4,3,2,1,0:T(8,128)(2,1)} %bitcast.27, bf16[4,8,48,512]{3,2,1,0:T(8,128)(2,1)} %copy-done.30, ...), custom_call_target="tpu_custom_call" | custom-call | bytes 40 | tf_op jit(solution)/shard_map/pair_sum/pallas_call | solution.py:49
  72.8 1.6 collective-permute-done.15.refs_4_
  74.4 1.3 finish.4
  75.7 7.9 %all-to-all-start.1 = ((f32[16,48,512]{2,1,0:T(8,128)}), f32[16,48,512]{2,1,0:T(8,128)S(1)}, u32[]{:S(2)}, u32[]{:S(2)}) async-start(f32[16,48,512]{2,1,0:T(8,128)} %get-tuple-element.103), calls=%async_computation.1 | async-start | bytes 3145728 | tf_op jit(solution)/shard_map/all_to_all | solution.py:381
  84.1 2.8 %collective-permute-start.13 = (f32[8,48,512]{2,1,0:T(8,128)}, f32[8,48,512]{2,1,0:T(8,128)S(1)}, u32[]{:S(2)}, u32[]{:S(2)}) collective-permute-start(f32[8,48,512]{2,1,0:T(8,128)} %copy-done.23), channel_id=1, source_target_pairs={{0,96},{16,112},{32,0},{48,16},{64,32},{80,48},{96,64},{112,80},{1... | collective-permute-start | bytes 2359304 | tf_op jit(solution)/shard_map/ppermute | solution.py:370
  86.9 3.2 %collective-permute-start.11 = (f32[4,48,512]{2,1,0:T(8,128)}, f32[4,48,512]{2,1,0:T(8,128)S(1)}, u32[]{:S(2)}, u32[]{:S(2)}) collective-permute-start(f32[4,48,512]{2,1,0:T(8,128)} %get-tuple-element.85), channel_id=1, source_target_pairs={{0,96},{16,112},{32,0},{48,16},{64,32},{80,48},{96,64},{112,80},{1... | collective-permute-start | bytes 1179656 | tf_op jit(solution)/shard_map/ppermute | solution.py:374
  90.1 15.4 %collective-permute-done.12.refs_1_.refs_3_ = f32[8,48,512]{2,1,0:T(8,128)S(1)} collective-permute-done((f32[8,48,512]{2,1,0:T(8,128)}, f32[8,48,512]{2,1,0:T(8,128)S(1)}, u32[]{:S(2)}, u32[]{:S(2)}) %collective-permute-start.12) | collective-permute-done | bytes 786464 | tf_op jit(solution)/shard_map/ppermute | solution.py:370
  107.4 3.7 %collective-permute-done.10.refs_2_ = f32[4,48,512]{2,1,0:T(8,128)S(1)} collective-permute-done((f32[4,48,512]{2,1,0:T(8,128)}, f32[4,48,512]{2,1,0:T(8,128)S(1)}, u32[]{:S(2)}, u32[]{:S(2)}) %collective-permute-start.10) | collective-permute-done | bytes 393248 | tf_op jit(solution)/shard_map/ppermute | solution.py:374
  111.1 1.3 finish.5
  112.4 6.9 %all-to-all-start.3 = ((f32[16,48,512]{2,1,0:T(8,128)}), f32[16,48,512]{2,1,0:T(8,128)S(1)}, u32[]{:S(2)}, u32[]{:S(2)}) async-start(f32[16,48,512]{2,1,0:T(8,128)} %get-tuple-element.106), calls=%async_computation.3 | async-start | bytes 3145728 | tf_op jit(solution)/shard_map/all_to_all | solution.py:381
  119.3 3.1 %collective-permute-start.8 = (f32[8,48,512]{2,1,0:T(8,128)}, f32[8,48,512]{2,1,0:T(8,128)S(1)}, u32[]{:S(2)}, u32[]{:S(2)}) collective-permute-start(f32[8,48,512]{2,1,0:T(8,128)} %copy-done.22), channel_id=1, source_target_pairs={{0,96},{16,112},{32,0},{48,16},{64,32},{80,48},{96,64},{112,80},{1... | collective-permute-start | bytes 2359304 | tf_op jit(solution)/shard_map/ppermute | solution.py:370
  122.5 3.4 %collective-permute-start.20 = (f32[4,48,512]{2,1,0:T(8,128)S(1)}, f32[4,48,512]{2,1,0:T(8,128)S(1)}, u32[]{:S(2)}, u32[]{:S(2)}) collective-permute-start(f32[4,48,512]{2,1,0:T(8,128)S(1)} %get-tuple-element.101), channel_id=1, source_target_pairs={{0,96},{16,112},{32,0},{48,16},{64,32},{80,48},{96,64},{112,80},{1... | collective-permute-start | bytes 1179656 | tf_op jit(solution)/shard_map/ppermute | solution.py:374
  125.9 14.5 %collective-permute-done.8.refs_3_.refs_1_ = f32[8,48,512]{2,1,0:T(8,128)S(1)} collective-permute-done((f32[8,48,512]{2,1,0:T(8,128)}, f32[8,48,512]{2,1,0:T(8,128)S(1)}, u32[]{:S(2)}, u32[]{:S(2)}) %collective-permute-start.8) | collective-permute-done | bytes 786464 | tf_op jit(solution)/shard_map/ppermute | solution.py:370
  140.4 3.3 %collective-permute-done.9.refs_1_.refs_3_ = f32[8,48,512]{2,1,0:T(8,128)S(1)} collective-permute-done((f32[8,48,512]{2,1,0:T(8,128)}, f32[8,48,512]{2,1,0:T(8,128)S(1)}, u32[]{:S(2)}, u32[]{:S(2)}) %collective-permute-start.9) | collective-permute-done | bytes 786464 | tf_op jit(solution)/shard_map/ppermute | solution.py:370
  143.7 1.4 copy-done.1
  146.7 4.2 %nesterov.3 = (f32[768,1024]{1,0:T(8,128)}, f32[768,1024]{1,0:T(8,128)}, f32[768,1024]{1,0:T(8,128)}, f32[768,768]{1,0:T(8,128)S(1)}, f32[8,128]{1,0:T(8,128)S(1)}) custom-call(s32[3]{0:T(128)S(1)} %pad_add_fusion.refs_0_, f32[768,512]{1,0:T(8,128)S(1)} %bitcast.16, f32[768,512]{1,0:T(8,128)S(1)} %bitcast.17, f32[768,1024]{1,0:T(8,128)} %bitcast.4.refs_3_, ...), custom_call_target="tpu_custom_call" | custom-call | bytes 60 | tf_op jit(solution)/shard_map/nesterov/pallas_call | solution.py:49
  150.9 1.4 copy-done.12
  152.4 1.3 finish.7
  153.7 7.0 %all-to-all-start.2 = ((f32[16,48,512]{2,1,0:T(8,128)}), f32[16,48,512]{2,1,0:T(8,128)S(1)}, u32[]{:S(2)}, u32[]{:S(2)}) async-start(f32[16,48,512]{2,1,0:T(8,128)} %get-tuple-element.105), calls=%async_computation.2 | async-start | bytes 3145728 | tf_op jit(solution)/shard_map/all_to_all | solution.py:381
  160.8 3.2 %collective-permute-start.18 = (f32[4,48,512]{2,1,0:T(8,128)S(1)}, f32[4,48,512]{2,1,0:T(8,128)S(1)}, u32[]{:S(2)}, u32[]{:S(2)}) collective-permute-start(f32[4,48,512]{2,1,0:T(8,128)S(1)} %copy-done.27), channel_id=1, source_target_pairs={{0,96},{16,112},{32,0},{48,16},{64,32},{80,48},{96,64},{112,80},{1... | collective-permute-start | bytes 1179656 | tf_op jit(solution)/shard_map/ppermute | solution.py:374
  164.0 6.0 %collective-permute-done.17.refs_2_ = f32[4,48,512]{2,1,0:T(8,128)S(1)} collective-permute-done((f32[4,48,512]{2,1,0:T(8,128)}, f32[4,48,512]{2,1,0:T(8,128)S(1)}, u32[]{:S(2)}, u32[]{:S(2)}) %collective-permute-start.17) | collective-permute-done | bytes 393248 | tf_op jit(solution)/shard_map/ppermute | solution.py:374
  173.4 1.2 finish.6
  174.6 2.4 all-to-all-done.2
  177.0 4.8 %all-to-all-start = ((f32[16,48,512]{2,1,0:T(8,128)}), f32[16,48,512]{2,1,0:T(8,128)}, u32[]{:S(2)}, u32[]{:S(2)}) async-start(f32[16,48,512]{2,1,0:T(8,128)} %get-tuple-element.98), calls=%async_computation | async-start | bytes 3145728 | tf_op jit(solution)/shard_map/all_to_all | solution.py:381
  181.8 5.3 %nesterov.4 = (f32[768,1024]{1,0:T(8,128)}, f32[768,1024]{1,0:T(8,128)}, f32[768,1024]{1,0:T(8,128)}, f32[768,768]{1,0:T(8,128)S(1)}, f32[8,128]{1,0:T(8,128)}) custom-call(s32[3]{0:T(128)S(1)} %pad_add_fusion.refs_0_, f32[768,512]{1,0:T(8,128)S(1)} %bitcast.12, f32[768,512]{1,0:T(8,128)S(1)} %bitcast.13, ...), custom_call_target="tpu_custom_call", output_to_operand_aliasing={{0}: (6, {}), {1}: (7, {}), {2}: (8, {})} | custom-call | bytes 60 | tf_op jit(solution)/shard_map/nesterov/pallas_call | solution.py:49
  187.1 1.4 copy-done.13
  188.5 5.3 %nesterov.5 = (f32[768,1024]{1,0:T(8,128)}, f32[768,1024]{1,0:T(8,128)}, f32[768,1024]{1,0:T(8,128)}, f32[768,768]{1,0:T(8,128)S(1)}, f32[8,128]{1,0:T(8,128)}) custom-call(s32[3]{0:T(128)S(1)} %pad_add_fusion.refs_0_, f32[768,512]{1,0:T(8,128)S(1)} %bitcast.14, f32[768,512]{1,0:T(8,128)S(1)} %bitcast.15, ...), custom_call_target="tpu_custom_call", output_to_operand_aliasing={{0}: (6, {}), {1}: (7, {}), {2}: (8, {})} | custom-call | bytes 60 | tf_op jit(solution)/shard_map/nesterov/pallas_call | solution.py:49
  193.8 1.4 copy-done.14
  195.3 2.7 %all-to-all-done = f32[16,48,512]{2,1,0:T(8,128)} async-done(((f32[16,48,512]{2,1,0:T(8,128)}), f32[16,48,512]{2,1,0:T(8,128)}, u32[]{:S(2)}, u32[]{:S(2)}) %all-to-all-start) | async-done | bytes 1572896 | tf_op jit(solution)/shard_map/all_to_all | solution.py:381
  198.0 36.0 %solve.1 = (f32[768,1024]{1,0:T(8,128)}, bf16[8,768,128]{2,1,0:T(8,128)(2,1)S(1)}, f32[8,128]{1,0:T(8,128)}) custom-call(s32[3]{0:T(128)S(1)} %pad_add_fusion.refs_0_, f32[768,512]{1,0:T(8,128)} %bitcast.5.refs_1_.refs_2_, f32[768,512]{1,0:T(8,128)} %bitcast.5.refs_1_.refs_2_, f32[768,1024]{1,0:T(8,128)} %bitcast.4.refs_3_, ...), custom_call_target="tpu_custom_call", output_to_operand_aliasing={{0}: (14, {})} | custom-call | bytes 400 | tf_op jit(solution)/shard_map/solve/pallas_call | solution.py:49
  234.0 31.7 %all_to_all.25 = bf16[128,48,128]{2,1,0:T(8,128)(2,1)S(1)} all-to-all(bf16[128,48,128]{2,1,0:T(8,128)(2,1)S(1)} %bitcast.19), channel_id=1, replica_groups=mesh['dp'=8,'expert'=16] {'dp','expert'}, dimensions={0} | all-to-all | bytes 3145728 | tf_op jit(solution)/shard_map/all_to_all | solution.py:409
  265.7 1.7 join.1
  (89 shorter events, 16.8 us)
Async XLA Ops:
  3.4 5.4 %collective-permute-start.1 = (bf16[4,8,48,512]{3,2,1,0:T(8,128)(2,1)S(1)}, bf16[4,8,48,512]{3,2,1,0:T(8,128)(2,1)S(1)}, u32[]{:S(2)}, u32[]{:S(2)}) collective-permute-start(bf16[4,8,48,512]{3,2,1,0:T(8,128)(2,1)S(1)} %get-tuple-element.64), channel_id=1, source_target_pairs={{0,16},{16,0},{32,48},{48,32},{64,80},{80,64},{96,112},{112,96},{1... | collective-permute-start | bytes 4718600 | tf_op jit(solution)/shard_map/ppermute | solution.py:365
  6.1 12.4 %collective-permute-start.4 = (bf16[4,8,48,512]{3,2,1,0:T(8,128)(2,1)S(1)}, bf16[4,8,48,512]{3,2,1,0:T(8,128)(2,1)}, u32[]{:S(2)}, u32[]{:S(2)}) collective-permute-start(bf16[4,8,48,512]{3,2,1,0:T(8,128)(2,1)S(1)} %get-tuple-element.68), channel_id=1, source_target_pairs={{0,16},{16,0},{32,48},{48,32},{64,80},{80,64},{96,112},{112,96},{1... | collective-permute-start | bytes 4718600 | tf_op jit(solution)/shard_map/ppermute | solution.py:365
  8.7 26.0 %collective-permute-start = (bf16[4,8,48,512]{3,2,1,0:T(8,128)(2,1)S(1)}, bf16[4,8,48,512]{3,2,1,0:T(8,128)(2,1)S(1)}, u32[]{:S(2)}, u32[]{:S(2)}) collective-permute-start(bf16[4,8,48,512]{3,2,1,0:T(8,128)(2,1)S(1)} %get-tuple-element.63), channel_id=1, source_target_pairs={{0,16},{16,0},{32,48},{48,32},{64,80},{80,64},{96,112},{112,96},{1... | collective-permute-start | bytes 4718600 | tf_op jit(solution)/shard_map/ppermute | solution.py:365
  8.8 1.1 copy-start.31
  13.3 21.3 %collective-permute-start.2 = (f32[8,48,512]{2,1,0:T(8,128)S(1)}, f32[8,48,512]{2,1,0:T(8,128)S(1)}, u32[]{:S(2)}, u32[]{:S(2)}) collective-permute-start(f32[8,48,512]{2,1,0:T(8,128)S(1)} %get-tuple-element.66), channel_id=1, source_target_pairs={{0,32},{16,48},{32,64},{48,80},{64,96},{80,112},{96,0},{112,16},{1... | collective-permute-start | bytes 2359304 | tf_op jit(solution)/shard_map/ppermute | solution.py:370
  14.9 19.7 %collective-permute-start.3 = (f32[8,48,512]{2,1,0:T(8,128)S(1)}, f32[8,48,512]{2,1,0:T(8,128)S(1)}, u32[]{:S(2)}, u32[]{:S(2)}) collective-permute-start(f32[8,48,512]{2,1,0:T(8,128)S(1)} %get-tuple-element.67), channel_id=1, source_target_pairs={{0,96},{16,112},{32,0},{48,16},{64,32},{80,48},{96,64},{112,80},{1... | collective-permute-start | bytes 2359304 | tf_op jit(solution)/shard_map/ppermute | solution.py:370
  16.5 94.6 %collective-permute-start.16 = (f32[768,1024]{1,0:T(8,128)}, f32[768,1024]{1,0:T(8,128)}, u32[]{:S(2)}, u32[]{:S(2)}) collective-permute-start(f32[768,1024]{1,0:T(8,128)} %bitcast.4.refs_3_), channel_id=1, source_target_pairs={{0,1},{1,0},{2,3},{3,2},{4,5},{5,4},{6,7},{7,6},{8,9},{9,8},{10,11... | collective-permute-start | bytes 9437192 | tf_op jit(solution)/shard_map/ppermute | solution.py:357
  34.7 1.1 copy-start.29
  40.4 2.1 copy-start.23
  42.5 24.6 %collective-permute-start.5 = (bf16[4,8,48,512]{3,2,1,0:T(8,128)(2,1)S(1)}, bf16[4,8,48,512]{3,2,1,0:T(8,128)(2,1)S(1)}, u32[]{:S(2)}, u32[]{:S(2)}) collective-permute-start(bf16[4,8,48,512]{3,2,1,0:T(8,128)(2,1)S(1)} %get-tuple-element.73), channel_id=1, source_target_pairs={{0,16},{16,0},{32,48},{48,32},{64,80},{80,64},{96,112},{112,96},{1... | collective-permute-start | bytes 4718600 | tf_op jit(solution)/shard_map/ppermute | solution.py:365
  42.6 21.6 %collective-permute-start.6 = (f32[8,48,512]{2,1,0:T(8,128)S(1)}, f32[8,48,512]{2,1,0:T(8,128)S(1)}, u32[]{:S(2)}, u32[]{:S(2)}) collective-permute-start(f32[8,48,512]{2,1,0:T(8,128)S(1)} %get-tuple-element.75), channel_id=1, source_target_pairs={{0,32},{16,48},{32,64},{48,80},{64,96},{80,112},{96,0},{112,16},{1... | collective-permute-start | bytes 2359304 | tf_op jit(solution)/shard_map/ppermute | solution.py:370
  44.2 21.7 %collective-permute-start.7 = (f32[8,48,512]{2,1,0:T(8,128)S(1)}, f32[8,48,512]{2,1,0:T(8,128)S(1)}, u32[]{:S(2)}, u32[]{:S(2)}) collective-permute-start(f32[8,48,512]{2,1,0:T(8,128)S(1)} %get-tuple-element.76), channel_id=1, source_target_pairs={{0,96},{16,112},{32,0},{48,16},{64,32},{80,48},{96,64},{112,80},{1... | collective-permute-start | bytes 2359304 | tf_op jit(solution)/shard_map/ppermute | solution.py:370
  45.9 26.9 %collective-permute-start.14 = (f32[4,48,512]{2,1,0:T(8,128)S(1)}, f32[4,48,512]{2,1,0:T(8,128)S(1)}, u32[]{:S(2)}, u32[]{:S(2)}) collective-permute-start(f32[4,48,512]{2,1,0:T(8,128)S(1)} %get-tuple-element.91), channel_id=1, source_target_pairs={{0,32},{16,48},{32,64},{48,80},{64,96},{80,112},{96,0},{112,16},{1... | collective-permute-start | bytes 1179656 | tf_op jit(solution)/shard_map/ppermute | solution.py:374
  64.2 10.2 %collective-permute-start.15 = (f32[4,48,512]{2,1,0:T(8,128)S(1)}, f32[4,48,512]{2,1,0:T(8,128)S(1)}, u32[]{:S(2)}, u32[]{:S(2)}) collective-permute-start(f32[4,48,512]{2,1,0:T(8,128)S(1)} %get-tuple-element.92), channel_id=1, source_target_pairs={{0,96},{16,112},{32,0},{48,16},{64,32},{80,48},{96,64},{112,80},{1... | collective-permute-start | bytes 1179656 | tf_op jit(solution)/shard_map/ppermute | solution.py:374
  65.9 1.2 copy-start.10
  67.1 1.1 copy-start.30
  72.8 2.9 %copy-start.21 = (f32[8,48,512]{2,1,0:T(8,128)}, f32[8,48,512]{2,1,0:T(8,128)S(1)}, u32[]{:S(2)}) copy-start(f32[8,48,512]{2,1,0:T(8,128)S(1)} %get-tuple-element.82) | copy-start | bytes 2359300
  72.8 2.9 %copy-start.22 = (f32[8,48,512]{2,1,0:T(8,128)}, f32[8,48,512]{2,1,0:T(8,128)S(1)}, u32[]{:S(2)}) copy-start(f32[8,48,512]{2,1,0:T(8,128)S(1)} %get-tuple-element.80) | copy-start | bytes 2359300
  75.7 36.7 %all-to-all-start.1 = ((f32[16,48,512]{2,1,0:T(8,128)}), f32[16,48,512]{2,1,0:T(8,128)S(1)}, u32[]{:S(2)}, u32[]{:S(2)}) async-start(f32[16,48,512]{2,1,0:T(8,128)} %get-tuple-element.103), calls=%async_computation.1 | async-start | bytes 3145728 | tf_op jit(solution)/shard_map/all_to_all | solution.py:381
  83.6 22.0 %collective-permute-start.12 = (f32[8,48,512]{2,1,0:T(8,128)}, f32[8,48,512]{2,1,0:T(8,128)S(1)}, u32[]{:S(2)}, u32[]{:S(2)}) collective-permute-start(f32[8,48,512]{2,1,0:T(8,128)} %copy-done.24), channel_id=1, source_target_pairs={{0,32},{16,48},{32,64},{48,80},{64,96},{80,112},{96,0},{112,16},{1... | collective-permute-start | bytes 2359304 | tf_op jit(solution)/shard_map/ppermute | solution.py:370
  84.1 21.4 %collective-permute-start.13 = (f32[8,48,512]{2,1,0:T(8,128)}, f32[8,48,512]{2,1,0:T(8,128)S(1)}, u32[]{:S(2)}, u32[]{:S(2)}) collective-permute-start(f32[8,48,512]{2,1,0:T(8,128)} %copy-done.23), channel_id=1, source_target_pairs={{0,96},{16,112},{32,0},{48,16},{64,32},{80,48},{96,64},{112,80},{1... | collective-permute-start | bytes 2359304 | tf_op jit(solution)/shard_map/ppermute | solution.py:370
  86.9 24.2 %collective-permute-start.10 = (f32[4,48,512]{2,1,0:T(8,128)}, f32[4,48,512]{2,1,0:T(8,128)S(1)}, u32[]{:S(2)}, u32[]{:S(2)}) collective-permute-start(f32[4,48,512]{2,1,0:T(8,128)} %get-tuple-element.84), channel_id=1, source_target_pairs={{0,32},{16,48},{32,64},{48,80},{64,96},{80,112},{96,0},{112,16},{1... | collective-permute-start | bytes 1179656 | tf_op jit(solution)/shard_map/ppermute | solution.py:374
  86.9 24.2 %collective-permute-start.11 = (f32[4,48,512]{2,1,0:T(8,128)}, f32[4,48,512]{2,1,0:T(8,128)S(1)}, u32[]{:S(2)}, u32[]{:S(2)}) collective-permute-start(f32[4,48,512]{2,1,0:T(8,128)} %get-tuple-element.85), channel_id=1, source_target_pairs={{0,96},{16,112},{32,0},{48,16},{64,32},{80,48},{96,64},{112,80},{1... | collective-permute-start | bytes 1179656 | tf_op jit(solution)/shard_map/ppermute | solution.py:374
  105.5 1.2 copy-start.4
  105.5 5.6 %copy-start.11 = (f32[8,48,512]{2,1,0:T(8,128)S(1)}, f32[8,48,512]{2,1,0:T(8,128)}, u32[]{:S(2)}) copy-start(f32[8,48,512]{2,1,0:T(8,128)} %copy-done.10) | copy-start | bytes 2359300
  105.6 5.6 %copy-start.20 = (f32[8,48,512]{2,1,0:T(8,128)S(1)}, f32[8,48,512]{2,1,0:T(8,128)}, u32[]{:S(2)}) copy-start(f32[8,48,512]{2,1,0:T(8,128)} %copy-done.19) | copy-start | bytes 2359300
  112.4 41.2 %all-to-all-start.3 = ((f32[16,48,512]{2,1,0:T(8,128)}), f32[16,48,512]{2,1,0:T(8,128)S(1)}, u32[]{:S(2)}, u32[]{:S(2)}) async-start(f32[16,48,512]{2,1,0:T(8,128)} %get-tuple-element.106), calls=%async_computation.3 | async-start | bytes 3145728 | tf_op jit(solution)/shard_map/all_to_all | solution.py:381
  119.3 21.1 %collective-permute-start.8 = (f32[8,48,512]{2,1,0:T(8,128)}, f32[8,48,512]{2,1,0:T(8,128)S(1)}, u32[]{:S(2)}, u32[]{:S(2)}) collective-permute-start(f32[8,48,512]{2,1,0:T(8,128)} %copy-done.22), channel_id=1, source_target_pairs={{0,96},{16,112},{32,0},{48,16},{64,32},{80,48},{96,64},{112,80},{1... | collective-permute-start | bytes 2359304 | tf_op jit(solution)/shard_map/ppermute | solution.py:370
  122.4 21.3 %collective-permute-start.9 = (f32[8,48,512]{2,1,0:T(8,128)}, f32[8,48,512]{2,1,0:T(8,128)S(1)}, u32[]{:S(2)}, u32[]{:S(2)}) collective-permute-start(f32[8,48,512]{2,1,0:T(8,128)} %copy-done.21), channel_id=1, source_target_pairs={{0,32},{16,48},{32,64},{48,80},{64,96},{80,112},{96,0},{112,16},{1... | collective-permute-start | bytes 2359304 | tf_op jit(solution)/shard_map/ppermute | solution.py:370
  122.4 30.0 %collective-permute-start.19 = (f32[4,48,512]{2,1,0:T(8,128)}, f32[4,48,512]{2,1,0:T(8,128)S(1)}, u32[]{:S(2)}, u32[]{:S(2)}) collective-permute-start(f32[4,48,512]{2,1,0:T(8,128)} %copy-done.25), channel_id=1, source_target_pairs={{0,32},{16,48},{32,64},{48,80},{64,96},{80,112},{96,0},{112,16},{1... | collective-permute-start | bytes 1179656 | tf_op jit(solution)/shard_map/ppermute | solution.py:374
  122.5 29.8 %collective-permute-start.20 = (f32[4,48,512]{2,1,0:T(8,128)S(1)}, f32[4,48,512]{2,1,0:T(8,128)S(1)}, u32[]{:S(2)}, u32[]{:S(2)}) collective-permute-start(f32[4,48,512]{2,1,0:T(8,128)S(1)} %get-tuple-element.101), channel_id=1, source_target_pairs={{0,96},{16,112},{32,0},{48,16},{64,32},{80,48},{96,64},{112,80},{1... | collective-permute-start | bytes 1179656 | tf_op jit(solution)/shard_map/ppermute | solution.py:374
  140.4 4.8 %copy-start.6 = (f32[8,48,512]{2,1,0:T(8,128)}, f32[8,48,512]{2,1,0:T(8,128)S(1)}, u32[]{:S(2)}) copy-start(f32[8,48,512]{2,1,0:T(8,128)S(1)} %collective-permute-done.8.refs_3_.refs_1_) | copy-start | bytes 2359300
  143.7 1.5 copy-start.8
  143.7 1.4 copy-start.1
  146.7 5.6 %copy-start.3 = (f32[8,48,512]{2,1,0:T(8,128)S(1)}, f32[8,48,512]{2,1,0:T(8,128)}, u32[]{:S(2)}) copy-start(f32[8,48,512]{2,1,0:T(8,128)} %copy-done.2) | copy-start | bytes 2359300
  146.7 5.6 %copy-start.5 = (f32[8,48,512]{2,1,0:T(8,128)S(1)}, f32[8,48,512]{2,1,0:T(8,128)}, u32[]{:S(2)}) copy-start(f32[8,48,512]{2,1,0:T(8,128)} %copy-done.4) | copy-start | bytes 2359300
  146.7 5.7 %copy-start.16 = (f32[8,48,512]{2,1,0:T(8,128)S(1)}, f32[8,48,512]{2,1,0:T(8,128)}, u32[]{:S(2)}) copy-start(f32[8,48,512]{2,1,0:T(8,128)} %copy-done.15) | copy-start | bytes 2359300
  150.9 1.4 copy-start.12
  153.7 7.1 %copy-start.27 = (f32[4,48,512]{2,1,0:T(8,128)S(1)}, f32[4,48,512]{2,1,0:T(8,128)}, u32[]{:S(2)}) copy-start(f32[4,48,512]{2,1,0:T(8,128)} %copy-done.26) | copy-start | bytes 1179652
  153.7 23.3 %all-to-all-start.2 = ((f32[16,48,512]{2,1,0:T(8,128)}), f32[16,48,512]{2,1,0:T(8,128)S(1)}, u32[]{:S(2)}, u32[]{:S(2)}) async-start(f32[16,48,512]{2,1,0:T(8,128)} %get-tuple-element.105), calls=%async_computation.2 | async-start | bytes 3145728 | tf_op jit(solution)/shard_map/all_to_all | solution.py:381
  160.7 9.3 %collective-permute-start.17 = (f32[4,48,512]{2,1,0:T(8,128)}, f32[4,48,512]{2,1,0:T(8,128)S(1)}, u32[]{:S(2)}, u32[]{:S(2)}) collective-permute-start(f32[4,48,512]{2,1,0:T(8,128)} %copy-done.28), channel_id=1, source_target_pairs={{0,32},{16,48},{32,64},{48,80},{64,96},{80,112},{96,0},{112,16},{1... | collective-permute-start | bytes 1179656 | tf_op jit(solution)/shard_map/ppermute | solution.py:374
  160.8 9.2 %collective-permute-start.18 = (f32[4,48,512]{2,1,0:T(8,128)S(1)}, f32[4,48,512]{2,1,0:T(8,128)S(1)}, u32[]{:S(2)}, u32[]{:S(2)}) collective-permute-start(f32[4,48,512]{2,1,0:T(8,128)S(1)} %copy-done.27), channel_id=1, source_target_pairs={{0,96},{16,112},{32,0},{48,16},{64,32},{80,48},{96,64},{112,80},{1... | collective-permute-start | bytes 1179656 | tf_op jit(solution)/shard_map/ppermute | solution.py:374
  169.9 1.1 copy-start.7
  171.1 1.1 copy-start.9
  172.2 1.1 copy-start.18
  177.0 21.0 %all-to-all-start = ((f32[16,48,512]{2,1,0:T(8,128)}), f32[16,48,512]{2,1,0:T(8,128)}, u32[]{:S(2)}, u32[]{:S(2)}) async-start(f32[16,48,512]{2,1,0:T(8,128)} %get-tuple-element.98), calls=%async_computation | async-start | bytes 3145728 | tf_op jit(solution)/shard_map/all_to_all | solution.py:381
  187.1 1.4 copy-start.13
  193.8 1.4 copy-start.14
  (9 other events, 7.6 us)

commit v2 on v1

--- a/solution.py
+++ b/solution.py
@@ -21,7 +21,7 @@
 sq_term = -4.775
 cube_term = 2.0315
 
-WIDTHS = (256, 256, 256, 256)
+WIDTHS = (384, 256, 256, 128)
 OFFSETS = tuple(sum(WIDTHS[:c]) for c in range(len(WIDTHS)))
 
 F32 = jnp.float32
@@ -30,7 +30,7 @@
 
 
 def call(kernel, inputs, in_specs, out_specs, out_shape, name,
-         after=(), grid=(), where=None, aliases=None, scratch=(), micros=2.0):
+         after=(), grid=(), where=None, aliases=None, scratch=(), mib=50):
     n, extra, outs = len(inputs), len(after), len(out_shape)
     lead = 0 if where is None else 1
 
@@ -51,10 +51,7 @@
         grid_spec=spec,
         out_shape=list(out_shape) + [jax.ShapeDtypeStruct((8, LANES), F32)],
         input_output_aliases={lead + k: v for k, v in (aliases or {}).items()},
-        compiler_params=pltpu.CompilerParams(vmem_limit_bytes=50 * MIB),
-        cost_estimate=pl.CostEstimate(
-            flops=0, bytes_accessed=int(micros * 10), transcendentals=0
-        ),
+        compiler_params=pltpu.CompilerParams(vmem_limit_bytes=mib * MIB),
         name=name,
     )(*(() if where is None else (where,)), *inputs, *after)
 
@@ -77,105 +74,38 @@
     return math.gcd(WIDTHS[c], OFFSETS[c], 256)
 
 
-def pack_kernel(where, g_ref, out_ref):
-    out_ref[...] = g_ref[:, 0]
-
-
-def pack(where, grads, c, after):
+def widen_kernel(g_ref, out_ref):
+    out_ref[...] = g_ref[...].astype(F32)
+
+
+def widen(grads, c, after):
     step = step_width(c)
     n, first, half = WIDTHS[c] // step, OFFSETS[c] // step, HALF // step
+    block = (32, ROWS, step)
     return call(
-        pack_kernel,
+        widen_kernel,
         [grads],
-        [
-            pl.BlockSpec(
-                (4, 1, 8, ROWS, step), lambda h, i, s: (0, 1 - s[0], 0, 0, h * half + first + i)
-            )
-        ],
-        [pl.BlockSpec((4, 8, ROWS, step), lambda h, i, s: (0, 0, 0, h * n + i))],
-        [jax.ShapeDtypeStruct((4, 8, ROWS, 2 * WIDTHS[c]), BF16)],
-        "pack", after, (2, n), where, micros=2.0 * WIDTHS[c] / 256,
-    )
-
-
-def pair_sum_kernel(where, g_ref, r_ref, up_ref, down_ref, acc_ref, own_ref):
-    y = where[1]
-
-    def total(k, rows):
-        k = lax.rem(k, 4)
-        return g_ref[k, 0, rows].astype(F32) + r_ref[k, rows].astype(F32)
-
-    for rows, up, down, acc in ((slice(0, 4), 2, 3, 1), (slice(4, 8), 1, 2, 3)):
-        own_ref[rows] = total(y, rows)
-        up_ref[rows] = total(y + up, rows)
-        down_ref[rows] = total(y + down, rows)
-        acc_ref[rows] = total(y + acc, rows)
-
-
-def pair_sum(where, grads, received, c, after):
-    step = step_width(c)
-    n, first, half = WIDTHS[c] // step, OFFSETS[c] // step, HALF // step
+        [pl.BlockSpec(block, lambda m, h, i: (m, 0, h * half + first + i))],
+        [pl.BlockSpec(block, lambda m, h, i: (m, 0, h * n + i))],
+        [jax.ShapeDtypeStruct((64, ROWS, 2 * WIDTHS[c]), F32)],
+        "widen", after, (2, 2, n),
+    )
+
+
+def double_kernel(g_ref, out_ref):
+    for j in range(4):
+        out_ref[2 * j] = g_ref[j]
+        out_ref[2 * j + 1] = g_ref[j]
+
+
+def double(summed, w, after):
     return call(
-        pair_sum_kernel,
-        [grads, received],
-        [
-            pl.BlockSpec(
-                (4, 1, 8, ROWS, step), lambda h, i, s: (0, s[0], 0, 0, h * half + first + i)
-            ),
-            pl.BlockSpec((4, 8, ROWS, step), lambda h, i, s: (0, 0, 0, h * n + i)),
-        ],
-        [pl.BlockSpec((8, ROWS, step), lambda h, i, s: (0, 0, h * n + i))] * 4,
-        [jax.ShapeDtypeStruct((8, ROWS, 2 * WIDTHS[c]), F32)] * 4,
-        "pair_sum", after, (2, n), where, micros=4.0 * WIDTHS[c] / 256,
-    )
-
-
-def relay_kernel(acc_up, u1_ref, acc_down, d1_ref, up_ref, down_ref):
-    up_ref[...] = acc_up[...] + u1_ref[...]
-    down_ref[...] = acc_down[...] + d1_ref[...]
-
-
-def relay(acc, u1, d1, w, after):
-    block = (2, ROWS, 2 * w)
-    low = pl.BlockSpec(block, lambda i: (i, 0, 0))
-    high = pl.BlockSpec(block, lambda i: (i + 2, 0, 0))
-    return call(
-        relay_kernel,
-        [acc, u1, acc, d1],
-        [low, low, high, high],
-        [low, low],
-        [jax.ShapeDtypeStruct((4, ROWS, 2 * w), F32)] * 2,
-        "relay", after, (2,), micros=1.0,
-    )
-
-
-def finish_kernel(own_ref, d1_ref, u2_ref, u1_ref, d2_ref, out_ref):
-    def write(a_ref, b_ref):
-        total = own_ref[...] + (a_ref[...] + b_ref[...])
-        for j in range(4):
-            out_ref[2 * j] = total[j]
-            out_ref[2 * j + 1] = total[j]
-
-    pl.when(pl.program_id(0) == 0)(lambda: write(d1_ref, u2_ref))
-    pl.when(pl.program_id(0) == 1)(lambda: write(u1_ref, d2_ref))
-
-
-def finish(own, d1, u2, u1, d2, w, after):
-    block = (4, ROWS, 2 * w)
-    held = pl.BlockSpec(block, lambda i: (0, 0, 0))
-    return call(
-        finish_kernel,
-        [own, d1, u2, u1, d2],
-        [
-            pl.BlockSpec(block, lambda i: (i, 0, 0)),
-            held,
-            held,
-            pl.BlockSpec(block, lambda i: (1, 0, 0)),
-            held,
-        ],
+        double_kernel,
+        [summed],
+        [pl.BlockSpec((4, ROWS, 2 * w), lambda i: (i, 0, 0))],
         [pl.BlockSpec((8, ROWS, 2 * w), lambda i: (i, 0, 0))],
         [jax.ShapeDtypeStruct((16, ROWS, 2 * w), F32)],
-        "finish", after, (2,), micros=1.0,
+        "double", after, (2,),
     )
 
 
@@ -207,8 +137,8 @@
     step = step_width(c)
     n, first = WIDTHS[c] // step, OFFSETS[c] // step
     block = (HID, step)
-    mine = pl.BlockSpec(block, lambda i, s: (0, s[2] * n + i))
-    theirs = pl.BlockSpec(block, lambda i, s: (0, (1 - s[2]) * n + i))
+    mine = pl.BlockSpec(block, lambda i, s: (0, s[0] * n + i))
+    theirs = pl.BlockSpec(block, lambda i, s: (0, (1 - s[0]) * n + i))
     place = pl.BlockSpec(block, lambda i, s: (0, first + i))
     whole = pl.BlockSpec((HID, HID), lambda i, s: (0, 0))
     wide = jax.ShapeDtypeStruct((HID, HALF), F32)
@@ -222,14 +152,13 @@
         [wide, wide, wide, jax.ShapeDtypeStruct((HID, HID), F32)],
         "nesterov", after, (n,), where,
         aliases={5: 0, 6: 1, 7: 2} if carried else {},
-        micros=6.0,
     )
 
 
 def solve_kernel(where, g_ref, gp_ref, m_ref, mp_ref, before_ref, *refs):
     own_refs, other_refs, refs = refs[:4], refs[4:8], refs[9:]
     new_ref, out_ref, gram_ref, last_own, last_other, *scratch = refs
-    h = where[2]
+    h = where[0]
     pairs = [scratch[2 * i : 2 * i + 2] for i in range(4)]
 
     new_ref[...], own = step_of(g_ref[...], m_ref[...])
@@ -297,15 +226,15 @@
     place = pl.BlockSpec(block, lambda i, s: (0, OFFSETS[c] // w))
     whole = pl.BlockSpec((HID, HID), lambda i, s: (0, 0))
     columns = [
-        pl.BlockSpec((HID, LANES), lambda i, s, k=k: (0, 2 * k + s[2])) for k in range(4)
+        pl.BlockSpec((HID, LANES), lambda i, s, k=k: (0, 2 * k + s[0])) for k in range(4)
     ]
     renewed, own, other, total = state
     return call(
         solve_kernel,
         [gradient, gradient, momentum, partner, total] + [own] * 4 + [other] * 4 + [renewed],
         [
-            pl.BlockSpec(block, lambda i, s: (0, s[2])),
-            pl.BlockSpec(block, lambda i, s: (0, 1 - s[2])),
+            pl.BlockSpec(block, lambda i, s: (0, s[0])),
+            pl.BlockSpec(block, lambda i, s: (0, 1 - s[0])),
             place,
             place,
             whole,
@@ -323,7 +252,6 @@
         scratch=[pltpu.VMEM((HID, HID), F32)]
         + [pltpu.VMEM(block, F32)] * 2
         + [pltpu.VMEM((HID, HID), BF16)] * 8,
-        micros=40.0,
     )
 
 
@@ -345,39 +273,23 @@
 
 
 def body(grad_parts, momentum):
-    dp, ex = lax.axis_index("dp"), lax.axis_index("expert")
-    where = jnp.stack([dp % 2, dp // 2, ex % 2]).astype(jnp.int32)
-    grads = grad_parts.reshape(4, 2, 8, ROWS, D)
+    where = jnp.full((1,), lax.axis_index("expert") % 2, jnp.int32)
+    grads = grad_parts[0]
     momentum = momentum[0]
-    core = [(i, i ^ 1) for i in range(8)]
-    upward = [(i, (i + 2) % 8) for i in range(8)]
-    downward = [(i, (i - 2) % 8) for i in range(8)]
-    partner = [(i, i ^ 1) for i in range(16)]
     n = len(WIDTHS)
-    theirs = lax.ppermute(momentum, "expert", partner)
-    received, sums, first, second, moved, token = ({} for _ in range(6))
+    theirs = lax.ppermute(momentum, "expert", [(i, i ^ 1) for i in range(16)])
+    sums, moved, token = {}, {}, {}
+    state = []
 
     def after(*steps):
         return [token[step] for step in steps if step in token]
 
-    def do_pack(c, *waits):
-        out, token["pack", c] = pack(where, grads, c, after(*waits))
-        received[c] = lax.ppermute(out, "dp", core)
-
-    def do_sum(c, *waits):
-        *sums[c], token["sum", c] = pair_sum(where, grads, received[c], c, after(*waits))
-        up, down = sums[c][:2]
-        first[c] = (lax.ppermute(up, "dp", upward), lax.ppermute(down, "dp", downward))
-
-    def do_relay(c, *waits):
-        up, down, token["relay", c] = relay(sums[c][2], *first[c], WIDTHS[c], after(*waits))
-        second[c] = (lax.ppermute(up, "dp", upward), lax.ppermute(down, "dp", downward))
-
-    def do_finish(c, *waits, arrays=()):
-        out, token["finish", c] = finish(
-            sums[c][3], first[c][1], second[c][0], first[c][0], second[c][1], WIDTHS[c],
-            after(*waits) + list(arrays),
-        )
+    def do_scatter(c, *waits):
+        out, token["widen", c] = widen(grads, c, after(*waits))
+        sums[c] = lax.psum_scatter(out, "dp", scatter_dimension=0, tiled=True)
+
+    def do_move(c, *waits):
+        out, token["double", c] = double(sums[c], WIDTHS[c], after(*waits))
         out = lax.all_to_all(out, "expert", split_axis=0, concat_axis=0, tiled=True)
         moved[c] = out.reshape(HID, -1)
 
@@ -386,25 +298,14 @@
             where, moved[c], momentum, theirs, state or None, c, after(*waits)
         )
 
-    state = []
-    do_pack(0)
-    do_pack(1)
-    do_sum(0)
-    do_sum(1)
-    do_pack(2)
-    do_relay(0, ("sum", 1), ("pack", 2))
-    do_sum(2, ("relay", 0))
+    do_scatter(0)
+    do_scatter(1, ("widen", 0))
+    do_scatter(2, ("widen", 1))
+    do_scatter(3, ("widen", 2))
     for c in range(n):
-        if c + 3 < n:
-            do_pack(c + 3, ("sum", c + 2))
-        if c + 1 < n:
-            do_relay(c + 1, ("sum", c + 2), ("pack", c + 3), ("finish", c - 1))
-        if c + 3 < n:
-            do_sum(c + 3, ("relay", c + 1))
-        last = () if c == n - 1 else (("nesterov", c - 2),)
-        do_finish(c, ("sum", c + 3), ("relay", c + 1), *last, arrays=[theirs] if c == 1 else ())
+        do_move(c, ("nesterov", c - 2))
         if c > 0:
-            do_nesterov(c - 1, ("finish", c))
+            do_nesterov(c - 1, ("double", c))
     renewed, update, _ = solve(where, moved[n - 1], momentum, theirs, state)
     update = lax.all_to_all(
         update.reshape(128, ROWS, LANES), ("dp", "expert"), split_axis=0, concat_axis=0, tiled=True

time: 271 us -> 316 us (1.17)
  waiting for transfers between devices: 80 us -> 157 us
  starting transfers between devices: 54.3 us -> 25.8 us
  between operations: 1.17 us -> 13.8 us
  local copies, waits for them, and re-layouts: 20.4 us -> 9.95 us
  Pallas kernels: 80 us -> 76.5 us
    reduce_scatter x0 -> x4, waiting for transfers between devices: none -> 75.3 us  [do_scatter(): sums[c] = lax.psum_scatter(out, 'dp', scatter_dimension=0, tiled=True)]
    ppermute x21 -> x1, starting transfers between devices: 27.7 us -> 1.88 us  [body(): theirs = lax.ppermute(momentum, 'expert', [(i, i ^ 1) for i in range(16)])]
    all_to_all x4, waiting for transfers between devices: 5.14 us -> 17.1 us  [do_move(): out = lax.all_to_all(out, 'expert', split_axis=0, concat_axis=0, tiled=True)]
    unnamed x64 -> x16, local copies, waits for them, and re-layouts: 20.4 us -> 9.95 us
    ppermute x21 -> x1, waiting for transfers between devices: 74.9 us -> 65 us  [body(): theirs = lax.ppermute(momentum, 'expert', [(i, i ^ 1) for i in range(16)])]
    pallas_call x21 -> x13, Pallas kernels: 80 us -> 76.5 us  [call(): pl.pallas_call(run, grid_spec=spec, out_shape=list(out_shape) + [jax.Shap...]
  transfers between devices with their start and end apart: 25 -> 9, of which waited for: 10 -> 5; matrix products, arithmetic and copies ran while one was open for 0% -> 0% of each run, Pallas kernels for 15% -> 13%
where the time goes in v2:
time: 316 us; the launch traced here: 315 us
  waiting for transfers between devices  157 us (50%)
  Pallas kernels  76.5 us (24%)
  blocking collectives  31.7 us (10%)
  starting transfers between devices  25.8 us (8%)
  between operations  13.8 us (4%)
  local copies, waits for them, and re-layouts  9.95 us (3%)
    pallas_call x13, Pallas kernels, call(): pl.pallas_call(run, grid_spec=spec, out_shape=list(out_shape) + [jax.Shap...  76.5 us
    reduce_scatter x4, waiting for transfers between devices, do_scatter(): sums[c] = lax.psum_scatter(out, 'dp', scatter_dimension=0, tiled=True)  75.3 us
    ppermute x1, waiting for transfers between devices, body(): theirs = lax.ppermute(momentum, 'expert', [(i, i ^ 1) for i in range(16)])  65 us
    all_to_all x1, blocking collectives, body(): lax.all_to_all(update.reshape(128, ROWS, LANES), ('dp', 'expert'), split_...  31.7 us
    all_to_all x4, starting transfers between devices, do_move(): out = lax.all_to_all(out, 'expert', split_axis=0, concat_axis=0, tiled=True)  23.8 us
    all_to_all x4, waiting for transfers between devices, do_move(): out = lax.all_to_all(out, 'expert', split_axis=0, concat_axis=0, tiled=True)  17.1 us
    unnamed x16, local copies, waits for them, and re-layouts  9.95 us
  transfers between devices with their start and end apart: 9, of which 5 were waited for; matrix products, arithmetic and copies ran while one was open for 0% of the time, Pallas kernels for 13%

profile of v2, /device:TPU:0, one launch (start us, length us, event | category | flops | bytes accessed | tf_op | source)
XLA Modules:
  0.0 315.2 jit_solution(14956629732357291223)
XLA Ops:
  7.2 0.0 reduce-scatter.9.cloned.1.call-start
  7.2 9.6 %widen.4 = (f32[64,48,768]{2,1,0:T(8,128)}, f32[8,128]{1,0:T(8,128)S(1)}) custom-call(bf16[64,48,2048]{2,1,0:T(8,128)(2,1)} %bitcast.18), custom_call_target="tpu_custom_call" | custom-call | tf_op jit(solution)/shard_map/widen/pallas_call | solution.py:49
  16.8 0.0 reduce-scatter.9.cloned.1.call-update
  16.9 0.0 reduce-scatter.7.cloned.1.call-start
  16.9 6.8 %widen.5 = (f32[64,48,512]{2,1,0:T(8,128)}, f32[8,128]{1,0:T(8,128)S(1)}) custom-call(bf16[64,48,2048]{2,1,0:T(8,128)(2,1)} %bitcast.19, f32[8,128]{1,0:T(8,128)S(1)} %get-tuple-element.33.refs_1_), custom_call_target="tpu_custom_call" | custom-call | tf_op jit(solution)/shard_map/widen/pallas_call | solution.py:49
  23.7 0.0 reduce-scatter.7.cloned.1.call-update
  23.7 0.0 reduce-scatter.11.cloned.1.call-start
  23.8 7.0 %widen.6 = (f32[64,48,512]{2,1,0:T(8,128)}, f32[8,128]{1,0:T(8,128)S(1)}) custom-call(bf16[64,48,2048]{2,1,0:T(8,128)(2,1)} %bitcast.20, f32[8,128]{1,0:T(8,128)S(1)} %get-tuple-element.34.refs_1_), custom_call_target="tpu_custom_call" | custom-call | tf_op jit(solution)/shard_map/widen/pallas_call | solution.py:49
  30.8 0.0 reduce-scatter.11.cloned.1.call-update
  30.8 0.0 reduce-scatter.5.cloned.1.call-start
  30.9 4.0 %widen.7 = (f32[64,48,256]{2,1,0:T(8,128)}, f32[8,128]{1,0:T(8,128)}) custom-call(bf16[64,48,2048]{2,1,0:T(8,128)(2,1)} %bitcast.21, f32[8,128]{1,0:T(8,128)S(1)} %get-tuple-element.35.refs_1_), custom_call_target="tpu_custom_call" | custom-call | tf_op jit(solution)/shard_map/widen/pallas_call | solution.py:49
  34.9 0.0 reduce-scatter.5.cloned.1.call-update
  35.0 42.0 %reduce-scatter.9.cloned.1.call-done.refs_0_ = f32[8,48,768]{2,1,0:T(8,128)} async-done(((f32[64,48,768]{2,1,0:T(8,128)}), f32[8,48,768]{2,1,0:T(8,128)}) %reduce-scatter.9.cloned.1.call-update) | async-done | bytes 1179664 | tf_op jit(solution)/shard_map/reduce_scatter | solution.py:289
  76.9 0.0 copy-start.4
  76.9 1.3 copy-done.4
  78.2 1.5 double.5
  79.7 7.0 %all-to-all-start.1 = ((f32[16,48,768]{2,1,0:T(8,128)}), f32[16,48,768]{2,1,0:T(8,128)}, u32[]{:S(2)}, u32[]{:S(2)}) async-start(f32[16,48,768]{2,1,0:T(8,128)} %get-tuple-element.40), calls=%async_computation.4 | async-start | bytes 4718592 | tf_op jit(solution)/shard_map/all_to_all | solution.py:293
  86.7 1.9 collective-permute-start
  88.5 33.4 %reduce-scatter.7.cloned.1.call-done.refs_0_ = f32[8,48,512]{2,1,0:T(8,128)} async-done(((f32[64,48,512]{2,1,0:T(8,128)}), f32[8,48,512]{2,1,0:T(8,128)}) %reduce-scatter.7.cloned.1.call-update) | async-done | bytes 786448 | tf_op jit(solution)/shard_map/reduce_scatter | solution.py:289
  121.9 0.0 copy-start.6
  121.9 1.1 copy-done.6
  123.0 1.2 double.4
  124.2 0.0 all-to-all-done.1
  124.2 6.8 %all-to-all-start = ((f32[16,48,512]{2,1,0:T(8,128)}), f32[16,48,512]{2,1,0:T(8,128)S(1)}, u32[]{:S(2)}, u32[]{:S(2)}) async-start(f32[16,48,512]{2,1,0:T(8,128)} %get-tuple-element.38), calls=%async_computation.2 | async-start | bytes 3145728 | tf_op jit(solution)/shard_map/all_to_all | solution.py:293
  131.0 65.0 %collective-permute-done.refs_4_ = f32[768,1024]{1,0:T(8,128)} collective-permute-done((f32[768,1024]{1,0:T(8,128)}, f32[768,1024]{1,0:T(8,128)}, u32[]{:S(2)}, u32[]{:S(2)}) %collective-permute-start) | collective-permute-done | bytes 3145760 | tf_op jit(solution)/shard_map/ppermute | solution.py:280
  196.0 6.9 %nesterov.3 = (f32[768,1024]{1,0:T(8,128)}, f32[768,1024]{1,0:T(8,128)}, f32[768,1024]{1,0:T(8,128)}, f32[768,768]{1,0:T(8,128)S(1)}, f32[8,128]{1,0:T(8,128)S(1)}) custom-call(s32[1]{0:T(128)} %bitcast.refs_0_, f32[768,768]{1,0:T(8,128)} %bitcast.4.refs_1_.refs_2_, f32[768,768]{1,0:T(8,128)} %bitcast.4.refs_1_.refs_2_, f32[768,1024]{1,0:T(8,128)} %bitcast.3.refs_3_, ...), custom_call_target="tpu_custom_call" | custom-call | tf_op jit(solution)/shard_map/nesterov/pallas_call | solution.py:49
  202.9 0.0 copy-start.1
  202.9 1.4 copy-done.1
  204.3 0.0 reduce-scatter.11.cloned.1.call-done.refs_0_
  204.3 0.0 copy-start.5
  204.3 1.1 copy-done.5
  205.4 0.1 double.6
  205.5 0.0 copy-start.3
  205.5 1.2 copy-done.3
  206.8 0.0 all-to-all-done
  206.8 6.2 %all-to-all-start.3 = ((f32[16,48,512]{2,1,0:T(8,128)}), f32[16,48,512]{2,1,0:T(8,128)S(1)}, u32[]{:S(2)}, u32[]{:S(2)}) async-start(f32[16,48,512]{2,1,0:T(8,128)} %copy-done.3), calls=%async_computation.7 | async-start | bytes 3145728 | tf_op jit(solution)/shard_map/all_to_all | solution.py:293
  213.0 5.8 %nesterov.4 = (f32[768,1024]{1,0:T(8,128)}, f32[768,1024]{1,0:T(8,128)}, f32[768,1024]{1,0:T(8,128)}, f32[768,768]{1,0:T(8,128)S(1)}, f32[8,128]{1,0:T(8,128)S(1)}) custom-call(s32[1]{0:T(128)} %bitcast.refs_0_, f32[768,512]{1,0:T(8,128)S(1)} %bitcast.10, f32[768,512]{1,0:T(8,128)S(1)} %bitcast.11, ...), custom_call_target="tpu_custom_call", output_to_operand_aliasing={{0}: (6, {}), {1}: (7, {}), {2}: (8, {})} | custom-call | tf_op jit(solution)/shard_map/nesterov/pallas_call | solution.py:49
  218.8 1.4 copy-done
  220.2 1.0 copy-done.7
  221.2 0.9 double.7
  222.1 12.6 %all-to-all-done.3 = f32[16,48,512]{2,1,0:T(8,128)S(1)} async-done(((f32[16,48,512]{2,1,0:T(8,128)}), f32[16,48,512]{2,1,0:T(8,128)S(1)}, u32[]{:S(2)}, u32[]{:S(2)}) %all-to-all-start.3) | async-done | bytes 1572896 | tf_op jit(solution)/shard_map/all_to_all | solution.py:293
  234.7 3.9 %all-to-all-start.2 = ((f32[16,48,256]{2,1,0:T(8,128)}), f32[16,48,256]{2,1,0:T(8,128)S(1)}, u32[]{:S(2)}, u32[]{:S(2)}) async-start(f32[16,48,256]{2,1,0:T(8,128)} %get-tuple-element.50), calls=%async_computation.6 | async-start | bytes 1572864 | tf_op jit(solution)/shard_map/all_to_all | solution.py:293
  238.6 5.8 %nesterov.5 = (f32[768,1024]{1,0:T(8,128)}, f32[768,1024]{1,0:T(8,128)}, f32[768,1024]{1,0:T(8,128)}, f32[768,768]{1,0:T(8,128)S(1)}, f32[8,128]{1,0:T(8,128)}) custom-call(s32[1]{0:T(128)} %bitcast.refs_0_, f32[768,512]{1,0:T(8,128)S(1)} %bitcast.12, f32[768,512]{1,0:T(8,128)S(1)} %bitcast.13, ...), custom_call_target="tpu_custom_call", output_to_operand_aliasing={{0}: (6, {}), {1}: (7, {}), {2}: (8, {})} | custom-call | tf_op jit(solution)/shard_map/nesterov/pallas_call | solution.py:49
  244.4 1.4 copy-done.2
  245.8 4.4 %all-to-all-done.2 = f32[16,48,256]{2,1,0:T(8,128)S(1)} async-done(((f32[16,48,256]{2,1,0:T(8,128)}), f32[16,48,256]{2,1,0:T(8,128)S(1)}, u32[]{:S(2)}, u32[]{:S(2)}) %all-to-all-start.2) | async-done | bytes 786464 | tf_op jit(solution)/shard_map/all_to_all | solution.py:293
  250.2 25.0 %solve.1 = (f32[768,1024]{1,0:T(8,128)}, bf16[8,768,128]{2,1,0:T(8,128)(2,1)S(1)}, f32[8,128]{1,0:T(8,128)}) custom-call(s32[1]{0:T(128)} %bitcast.refs_0_, f32[768,256]{1,0:T(8,128)S(1)} %bitcast.14, f32[768,256]{1,0:T(8,128)S(1)} %bitcast.15, f32[768,1024]{1,0:T(8,128)} %bitcast.3.refs_3_, ...), custom_call_target="tpu_custom_call", output_to_operand_aliasing={{0}: (14, {})} | custom-call | tf_op jit(solution)/shard_map/solve/pallas_call | solution.py:49
  275.2 31.7 %all_to_all.25 = bf16[128,48,128]{2,1,0:T(8,128)(2,1)S(1)} all-to-all(bf16[128,48,128]{2,1,0:T(8,128)(2,1)S(1)} %bitcast.17), channel_id=1, replica_groups=mesh['dp'=8,'expert'=16] {'dp','expert'}, dimensions={0} | all-to-all | bytes 3145728 | tf_op jit(solution)/shard_map/all_to_all | solution.py:310
  306.9 1.7 join.1
  (4 shorter events, 0.0 us)
Async XLA Ops:
  7.2 69.8 %reduce-scatter.9.cloned.1.call-start = ((), (), s32[]{:S(2)}) async-start(), calls=%async_computation.11 | async-start | bytes 10616832 | tf_op jit(solution)/shard_map/reduce_scatter | solution.py:289
  16.9 105.0 %reduce-scatter.7.cloned.1.call-start = ((), (), s32[]{:S(2)}) async-start(), calls=%async_computation.10 | async-start | bytes 7077888 | tf_op jit(solution)/shard_map/reduce_scatter | solution.py:289
  23.7 180.5 %reduce-scatter.11.cloned.1.call-start = ((), (), s32[]{:S(2)}) async-start(), calls=%async_computation.12 | async-start | bytes 7077888 | tf_op jit(solution)/shard_map/reduce_scatter | solution.py:289
  30.8 189.3 %reduce-scatter.5.cloned.1.call-start = ((), (), s32[]{:S(2)}) async-start(), calls=%async_computation.9 | async-start | bytes 3538944 | tf_op jit(solution)/shard_map/reduce_scatter | solution.py:289
  76.9 1.3 copy-start.4
  79.7 44.5 %all-to-all-start.1 = ((f32[16,48,768]{2,1,0:T(8,128)}), f32[16,48,768]{2,1,0:T(8,128)}, u32[]{:S(2)}, u32[]{:S(2)}) async-start(f32[16,48,768]{2,1,0:T(8,128)} %get-tuple-element.40), calls=%async_computation.4 | async-start | bytes 4718592 | tf_op jit(solution)/shard_map/all_to_all | solution.py:293
  86.7 109.3 %collective-permute-start = (f32[768,1024]{1,0:T(8,128)}, f32[768,1024]{1,0:T(8,128)}, u32[]{:S(2)}, u32[]{:S(2)}) collective-permute-start(f32[768,1024]{1,0:T(8,128)} %bitcast.3.refs_3_), channel_id=1, source_target_pairs={{0,1},{1,0},{2,3},{3,2},{4,5},{5,4},{6,7},{7,6},{8,9},{9,8},{10,11... | collective-permute-start | bytes 9437192 | tf_op jit(solution)/shard_map/ppermute | solution.py:280
  121.9 1.1 copy-start.6
  124.2 82.6 %all-to-all-start = ((f32[16,48,512]{2,1,0:T(8,128)}), f32[16,48,512]{2,1,0:T(8,128)S(1)}, u32[]{:S(2)}, u32[]{:S(2)}) async-start(f32[16,48,512]{2,1,0:T(8,128)} %get-tuple-element.38), calls=%async_computation.2 | async-start | bytes 3145728 | tf_op jit(solution)/shard_map/all_to_all | solution.py:293
  202.9 1.4 copy-start.1
  204.3 1.1 copy-start.5
  205.5 1.2 copy-start.3
  206.8 27.9 %all-to-all-start.3 = ((f32[16,48,512]{2,1,0:T(8,128)}), f32[16,48,512]{2,1,0:T(8,128)S(1)}, u32[]{:S(2)}, u32[]{:S(2)}) async-start(f32[16,48,512]{2,1,0:T(8,128)} %copy-done.3), calls=%async_computation.7 | async-start | bytes 3145728 | tf_op jit(solution)/shard_map/all_to_all | solution.py:293
  218.8 1.4 copy-start
  220.2 1.0 copy-start.7
  234.7 15.5 %all-to-all-start.2 = ((f32[16,48,256]{2,1,0:T(8,128)}), f32[16,48,256]{2,1,0:T(8,128)S(1)}, u32[]{:S(2)}, u32[]{:S(2)}) async-start(f32[16,48,256]{2,1,0:T(8,128)} %get-tuple-element.50), calls=%async_computation.6 | async-start | bytes 1572864 | tf_op jit(solution)/shard_map/all_to_all | solution.py:293
  244.4 1.4 copy-start.2
Sparse Core Ops, SparseCore 0:
  17.0 59.8 reduce-scatter.8
  79.3 42.5 reduce-scatter.6
  124.3 42.0 reduce-scatter.10
  168.7 35.5 reduce-scatter.4
